TPU v7x, 32 devices: a whole 2x2x4 slice. The times are simulated.
32 devices in a mesh: fsdp: 4 (over z), replica: 4 (over y, core), tm: 2 (over x).
Axes of the slice: x: 2, y: 2, z: 4, core: 2. Of those that a mesh axis runs over, the one named last changes fastest.
Arguments:
- clip_input: bfloat16 [4, 8, 16, 16, 512], P('replica', 'tm'), may hold values from -6 to 6
- first_kernel: bfloat16 [27, 512, 512], P(None, None, 'fsdp'), may hold values from -0.0546875 to 0.0546875
- second_kernel: bfloat16 [27, 512, 512], P(None, 'fsdp'), may hold values from -0.0546875 to 0.0546875
- out_grad: bfloat16 [4, 2, 4, 4, 512], P('replica', 'tm'), may hold values from -2 to 2
- tap_mix: float32 [2, 27, 27], replicated, may hold values from -0.14 to 1.4
- left_panels: float32 [2, 512, 512], P(None, 'fsdp'), may hold values from -0.05 to 2
- right_panels: float32 [2, 512, 512], P(None, 'fsdp', ('replica', 'tm')), may hold values from -0.05 to 2
Outputs:
- update: bfloat16 [2, 27, 512, 512], P(None, None, 'fsdp', ('replica', 'tm'))
All inputs are finite; a program needn't handle non-finite values.
Results may differ from a plain program's by a relative error of at most 0.0049.
Values may be sent and summed in bfloat16 or wider, within the bound.
No kernel may reach another device: no remote copies, remote signals or barrier semaphores. Data moves between devices by JAX's collectives and lax.ppermute only.
A program may use at most 128 MiB of HBM per device.

v0:
```python
import functools

import jax
import jax.numpy as jnp
import numpy as np
from jax import lax
from jax.experimental import pallas as pl
from jax.experimental.pallas import tpu as pltpu
from jax.sharding import Mesh, PartitionSpec as P

TAPS = 27
F32, BF16 = jnp.float32, jnp.bfloat16
ROOM = 50 << 20
PROJECT_COST = 16 << 20
HIDDEN_COST = 200 << 20
NT = (((1,), (1,)), ((), ()))
VMEM = pl.BlockSpec(memory_space=pltpu.VMEM)
HBM = pl.BlockSpec(memory_space=pltpu.HBM)
SMEM = pl.BlockSpec(memory_space=pltpu.SMEM)
ANY = pl.BlockSpec(memory_space=pl.ANY)


def shifted(block, axis, distance):
    devices = range(lax.axis_size(axis))
    route = [(i - distance, i) for i in devices if i - distance in devices]
    return lax.ppermute(block, axis, route)


def dot(left, right):
    return jnp.dot(left, right, preferred_element_type=F32)


def dot_nt(left, right):
    return lax.dot_general(left, right, NT, preferred_element_type=F32)


def quotient(value, size):
    return value >> (size.bit_length() - 1) if size & (size - 1) == 0 else value // size


def remainder(value, size):
    return value & (size - 1) if size & (size - 1) == 0 else value % size


def halves(value):
    high = value.astype(BF16)
    return high, (value - high.astype(F32)).astype(BF16)


def column_picks(side):
    half = side // 2
    picks = np.zeros((2, half, half, half, side), np.float32)
    for row in range(half):
        for x in range(side):
            picks[x % 2, row, x // 2, row, x] = 1
    return picks.reshape(half * side, half * side)


def spread_picks(half):
    quarter = half // 2
    picks = np.zeros((3, 3, half, half, quarter, quarter), np.float32)
    for b in range(3):
        for c in range(3):
            for out_y in range(quarter):
                for out_x in range(quarter):
                    y, x = 2 * out_y + b - 1, 2 * out_x + c - 1
                    if y >= 0 and x >= 0:
                        picks[b, c, y, x, out_y, out_x] = 1
    return picks.reshape(9 * half * half, quarter * quarter)


def parity_rows(lines, pick):
    rows = dot(pick, lines).astype(BF16)
    cells = rows.shape[0] // 2
    return rows[:cells], rows[cells:]


def folded_taps(rows, weights, shift_ref, half):
    sums = {}
    for line, column in np.ndindex(2, 2):
        taps = [(b, c) for b in ((2, 0) if line else (1,)) for c in ((2, 0) if column else (1,))]
        product = dot(rows(line, column), jnp.concatenate([weights(*tap) for tap in taps], axis=1))
        wide = product.shape[1] // len(taps)
        for at, (b, c) in enumerate(taps):
            part = product[:, at * wide : (at + 1) * wide]
            key = (int(b == 0), int(c == 0))
            sums[key] = sums[key] + part if key in sums else part
    total = sums.pop((0, 0))
    count, wide = total.shape
    pad = shift_ref.shape[1] - count
    places = lax.broadcasted_iota(jnp.int32, (count, wide), 0)
    row = remainder(quotient(places, half), half)
    column = remainder(places, half)
    for at, ((dr, dc), part) in enumerate(sums.items()):
        shift_ref[at, pl.ds(pad, count), :] = part
        moved = shift_ref[at, pl.ds(pad - (dr * half + dc), count), :]
        total += jnp.where((row >= dr) & (column >= dc), moved, 0.0)
    return total


def project_kernel(
    x_any, left_any, grad_any, pick_any, first_any,
    out_ref, halo_ref, x_ref, left_ref, grad_ref, pick_ref, first_ref, rows_ref, shift_ref, arrived,
):
    frames, half, _, side, channels = x_ref.shape
    order = [frame for time in (1, 0) for frame in range(time, frames, 2)]
    pairs_of = [
        (left_any.at[0], left_ref),
        (x_any.at[order[0]], x_ref.at[order[0]]),
        (x_any.at[order[1]], x_ref.at[order[1]]),
        (pick_any, pick_ref),
        (first_any.at[pl.ds(0, 9)], first_ref),
        (x_any.at[order[2]], x_ref.at[order[2]]),
        (x_any.at[order[3]], x_ref.at[order[3]]),
        (grad_any, grad_ref),
    ]
    copies = [
        pltpu.make_async_copy(source, target, arrived.at[at])
        for at, (source, target) in enumerate(pairs_of)
    ]
    for copy in copies:
        copy.start()
    wide = left_ref.shape[0]
    pairs = frames // 2
    size = pairs * half * side
    target = lax.broadcasted_iota(jnp.int32, (size, size), 0)
    source = lax.broadcasted_iota(jnp.int32, (size, size), 1)
    cells = size // 2
    wanted = 2 * remainder(target, cells) + quotient(target, cells)
    pick = jnp.where(source == wanted, 1.0, 0.0).astype(BF16)
    copies[0].wait()
    both = jnp.concatenate(halves(left_ref[...]), axis=0)

    def project(time):
        for row in range(2):
            block = jnp.concatenate(
                [
                    x_ref[frame, :, row].reshape(half * side, channels)
                    for frame in range(time, frames, 2)
                ],
                axis=0,
            )
            full = dot_nt(block, both)
            small = (full[:, :wide] + full[:, wide:]).astype(BF16)
            ordered = dot(pick, small).astype(BF16)
            at = (4 * time + 2 * row) * cells
            out_ref[at : at + size, :] = ordered

    copies[1].wait()
    copies[2].wait()
    project(1)
    copies[3].wait()
    classes = [
        parity_rows(x_ref[frames - 1, :, line].reshape(half * side, channels), pick_ref[...])
        for line in range(2)
    ]
    copies[4].wait()
    halo_ref[pl.ds(0, half * half), :] = folded_taps(
        lambda line, column: classes[line][column],
        lambda b, c: first_ref[3 * b + c],
        shift_ref,
        half,
    )
    copies[5].wait()
    copies[6].wait()
    project(0)
    copies[7].wait()
    grad_rows = stacked_rows(grad_ref, rows_ref)
    count = grad_rows.shape[0]
    for block in range(channels // wide):
        at = 8 * cells + block * count
        out_ref[at : at + count, :] = grad_rows[:, block * wide : (block + 1) * wide]
        at = half * half + block * count
        halo_ref[at : at + count, :] = rows_ref[:, block * wide : (block + 1) * wide]


def stacked_rows(grad_ref, rows_ref):
    quarter = grad_ref.shape[0]
    for row in range(quarter):
        rows_ref[pl.ds(row * quarter, quarter), :] = grad_ref[row].astype(F32)
    return rows_ref[...].astype(BF16)


def transposed_products(rows, kernel, taps):
    total = dot_nt(rows[0], kernel[taps[0]])
    for at in range(1, len(taps)):
        total += dot_nt(rows[at], kernel[taps[at]])
    return total


def spread_rows(picks_ref, rows, cells):
    spread = dot(picks_ref[...], rows).astype(BF16)
    return [spread[tap * cells : (tap + 1) * cells] for tap in range(9)]


def hidden_kernel(
    tm_ref, x_ref, prior_ref, grad_ref, later_ref, pick_ref, spread_ref,
    first_any, second_any, out_ref, rows_ref, classes, first, second, shift_ref, arrived, *,
    clip_parts,
):
    frames, half, _, side, channels = x_ref.shape
    cells = half * half
    has_prior = jnp.where(tm_ref[0] > 0, 1.0, 0.0)
    has_later = jnp.where(tm_ref[0] < clip_parts - 1, 1.0, 0.0)
    copies = {
        (at, a): pltpu.make_async_copy(
            source.at[pl.ds(9 * a, 9)], target.at[pl.ds(9 * a, 9)], arrived.at[at, a]
        )
        for at, (source, target) in enumerate(((second_any, second), (first_any, first)))
        for a in (1, 2, 0)
    }
    for copy in copies.values():
        copy.start()
    own_rows = stacked_rows(grad_ref, rows_ref)
    own = spread_rows(spread_ref, own_rows, cells)
    copies[0, 1].wait()
    copies[0, 2].wait()
    both = None
    for tap in range(9):
        pair = jnp.concatenate([second[9 + tap], second[18 + tap]], axis=0)
        term = dot_nt(own[tap], pair)
        both = term if both is None else both + term
    early, late = both[:, : second.shape[1]], both[:, second.shape[1] :]
    for frame in range(frames):
        for line in range(2):
            lines = x_ref[frame, :, line].reshape(half * side, channels)
            classes[frame, line, 0], classes[frame, line, 1] = parity_rows(lines, pick_ref[...])
    count = own_rows.shape[0]
    wide = first.shape[2]
    later_rows = jnp.concatenate(
        [
            later_ref[pl.ds(cells + count * block, count), :]
            for block in range(channels // wide)
        ],
        axis=1,
    )
    after = spread_rows(spread_ref, later_rows.astype(BF16), cells)
    copies[0, 0].wait()
    late += transposed_products(after, second, range(9)) * has_later
    hidden_grad = jnp.concatenate([early, late], axis=0)
    nothing = jnp.zeros((cells, channels), BF16)

    def rows_of(line, column):
        held = [classes[frame, line, column] for frame in range(frames)]
        return jnp.concatenate(
            [
                jnp.concatenate([nothing, held[0], held[1]], axis=1),
                jnp.concatenate([held[1], held[2], held[3]], axis=1),
            ],
            axis=0,
        )

    for a in (1, 2, 0):
        copies[1, a].wait()
    pre = folded_taps(
        rows_of,
        lambda b, c: jnp.concatenate([first[9 * a + 3 * b + c] for a in range(3)], axis=0),
        shift_ref,
        half,
    )
    pre += jnp.concatenate(
        [prior_ref[pl.ds(0, cells), :] * has_prior, jnp.zeros((cells, wide), F32)], axis=0
    )
    sig = jax.nn.sigmoid(pre)
    hidden = (pre * sig).astype(BF16)
    pre_grad = (hidden_grad * sig * (1.0 + pre * (1.0 - sig))).astype(BF16)
    groups, slices, _, share, _ = out_ref.shape
    for at in range(slices):
        place = slice(at * share, (at + 1) * share)
        for group in range(groups):
            out_ref[group, at, 0] = pre_grad[place]
            out_ref[group, at, 1] = hidden[place]


def right_kernel(place_ref, core_ref, *refs, cores):
    acts_refs, right_refs, out_ref = refs[:cores], refs[cores:-1], refs[-1]
    parts, slices = acts_refs[0].shape[:2]
    width = right_refs[0].shape[1]
    for layer in range(2):
        rights = [jnp.concatenate(halves(ref[layer]), axis=0) for ref in right_refs]
        for cross, acts_ref in enumerate(acts_refs):
            total = None
            for distance in range(slices):
                origin = lax.rem(place_ref[0] + (slices - distance), slices)
                rows = jnp.concatenate(
                    [acts_ref[part, origin, layer] for part in range(parts)], axis=0
                )
                term = dot_nt(rights[distance], rows)
                total = term if total is None else total + term
            core = lax.rem(core_ref[0] + cross, cores)
            out_ref[core, pl.ds(layer * width, width), :] = (total[:width] + total[width:]).astype(
                BF16
            )


def tables_kernel(after_any, mix_ref, shift_ref, sort_ref, mixers_ref, *, slices, clip_parts, half):
    del after_any
    size = shift_ref.shape[0]
    cells = size // clip_parts
    share = cells // slices
    frames = size // (half * half)
    held = lax.broadcasted_iota(jnp.int32, (size, size), 0)
    cell = lax.broadcasted_iota(jnp.int32, (size, size), 1)
    part = remainder(quotient(held, share), clip_parts)
    slot = quotient(held, share * clip_parts)
    natural = part * cells + slot * share + remainder(held, share)
    frame = quotient(cell, half * half)
    row = remainder(quotient(cell, half), half)
    column = remainder(cell, half)
    for shift in range(8):
        dt, dr, dc = shift // 4, shift // 2 % 2, shift % 2
        found = natural == cell + ((dt * half + dr) * half + dc)
        if dt:
            found &= frame < frames - 1
        if dr:
            found &= row < half - 1
        if dc:
            found &= column < half - 1
        shift_ref[:, pl.ds(shift * size, size)] = jnp.where(found, 1.0, 0.0).astype(BF16)
    quarter = half // 2
    outputs = size // 8
    kind = quotient(cell, outputs)
    frame = 2 * remainder(quotient(cell, quarter * quarter), frames // 2) + quotient(kind, 4)
    row = 2 * remainder(quotient(cell, quarter), quarter) + remainder(quotient(kind, 2), 2)
    column = 2 * remainder(cell, quarter) + remainder(kind, 2)
    found = natural == (frame * half + row) * half + column
    sort_ref[...] = jnp.where(found, 1.0, 0.0).astype(BF16)

    count = mixers_ref.shape[2]
    tap = lax.broadcasted_iota(jnp.int32, (count, TAPS), 1)
    line = lax.broadcasted_iota(jnp.int32, (count, TAPS), 0)
    spread = jnp.where(quotient(line, 8) == tap, 1.0, 0.0).astype(BF16)
    lines = lax.broadcasted_iota(jnp.int32, (count, count), 0)
    others = lax.broadcasted_iota(jnp.int32, (count, count), 1)
    same = remainder(lines, 8) == remainder(others, 8)
    for layer in range(2):
        for at, part in enumerate(halves(mix_ref[layer])):
            wider = dot_nt(dot(spread, part).astype(BF16), spread)
            mixers_ref[layer, at] = jnp.where(same, wider, 0.0).astype(BF16)


def update_kernel(
    place_ref, chip_ref, core_ref, tm_ref, *refs, slices, cores, clip_parts, half
):
    columns_refs, piece_refs = refs[:slices], refs[slices : slices + cores]
    (
        left_ref, mixers_ref, shift_ref, sort_ref,
        out_ref, left_rows_ref, columns, shifts, grads, raw, arrived,
    ) = refs[slices + cores :]
    parts = left_rows_ref.shape[0]
    chips = parts // (cores * clip_parts)
    copies = []
    for cross, piece_ref in enumerate(piece_refs):
        core = lax.rem(core_ref[0] + cross, cores)
        for at, (step, turn) in enumerate(np.ndindex(chips, clip_parts)):
            chip = lax.rem(chip_ref[0] + (chips - step), chips)
            place = lax.rem(tm_ref[0] + (clip_parts - turn), clip_parts)
            target = left_rows_ref.at[(chip * cores + core) * clip_parts + place]
            copies.append(
                pltpu.make_async_copy(piece_ref.at[at], target, arrived.at[len(copies)])
            )
    for copy in copies:
        copy.start()
    for distance in range(slices):
        origin = lax.rem(place_ref[0] + (slices - distance), slices)
        columns[origin] = columns_refs[distance][...]
    wide, channels = left_ref.shape[1:]
    width = columns.shape[2] // 2
    clips = parts // clip_parts
    share = columns.shape[3] // chips
    clip_cells = slices * share
    cells = clip_cells // clip_parts
    frames = clip_cells // (half * half)
    outputs = clip_cells // 8

    def by_clip(layer):
        return jnp.concatenate(
            [
                jnp.concatenate(
                    [
                        columns[
                            at, clip % cores, pl.ds(layer * width, width),
                            pl.ds(clip // cores * share, share),
                        ]
                        for at in range(slices)
                    ],
                    axis=1,
                )
                for clip in range(clips)
            ],
            axis=0,
        )

    first = by_clip(0)
    for shift in range(8):
        moved = dot(first, shift_ref[:, pl.ds(shift * clip_cells, clip_cells)]).astype(BF16)
        for clip in range(clips):
            shifts[shift, clip] = moved[clip * width : (clip + 1) * width]
    second = dot(by_clip(1), sort_ref[...]).astype(BF16)

    for copy in copies:
        copy.wait()
    own_outputs = outputs // clip_parts
    blocks = channels // wide
    out_grad = jnp.concatenate(
        [
            jnp.concatenate(
                [
                    left_rows_ref[part, pl.ds(8 * cells + own_outputs * at, own_outputs), :]
                    for at in range(blocks)
                ],
                axis=1,
            )
            for part in range(parts)
        ],
        axis=0,
    )
    full = dot_nt(out_grad, jnp.concatenate(halves(left_ref[1]), axis=0))
    total = parts * own_outputs
    quarter = half // 2
    grads[pl.ds(0, total), :] = full[:, :wide] + full[:, wide:]
    places = lax.broadcasted_iota(jnp.int32, (total, wide), 0)
    frame = remainder(quotient(places, quarter * quarter), frames // 2)
    row = remainder(quotient(places, quarter), quarter)
    column = remainder(places, quarter)
    second_rows = []
    for shift in range(8):
        dt, dr, dc = shift // 4, shift // 2 % 2, shift % 2
        moved = grads[pl.ds((dt * quarter + dr) * quarter + dc, total), :]
        inside = (frame + dt < frames // 2) & (row + dr < quarter) & (column + dc < quarter)
        second_rows.append(jnp.where(inside, moved, 0.0).astype(BF16))

    for time, line in np.ndindex(2, 2):
        even = [
            (9 * a + 3 * b + 1, 4 * (a == 0) + 2 * (b == 0))
            for a in ((0, 2) if time else (1,))
            for b in ((0, 2) if line else (1,))
        ]
        odd = [(tap + 1, shift) for tap, shift in even] + [
            (tap - 1, shift + 1) for tap, shift in even
        ]
        kind = 4 * time + 2 * line
        sums = None
        for clip in range(clips):
            left = jnp.concatenate([shifts[shift, clip] for _, shift in odd], axis=0)
            rows = jnp.concatenate(
                [
                    jnp.concatenate(
                        [
                            left_rows_ref[
                                clip * clip_parts + part, pl.ds((kind + at) * cells, cells), :
                            ]
                            for part in range(clip_parts)
                        ],
                        axis=0,
                    )
                    for at in range(2)
                ],
                axis=1,
            )
            term = dot(left, rows)
            sums = term if sums is None else sums + term
        for at, (tap, _) in enumerate(even):
            raw[0, tap] = sums[at * width : (at + 1) * width, :wide]
        for at, (tap, _) in enumerate(odd):
            raw[0, tap] = sums[at * width : (at + 1) * width, wide:]
        for place, taps in enumerate((even, odd)):
            chosen = jnp.concatenate(
                [
                    second[
                        clip * width : (clip + 1) * width,
                        (kind + place) * outputs : (kind + place + 1) * outputs,
                    ]
                    for clip in range(clips)
                ],
                axis=1,
            )
            products = dot(
                chosen, jnp.concatenate([second_rows[shift] for _, shift in taps], axis=1)
            )
            for at, (tap, _) in enumerate(taps):
                raw[1, tap] = products[:, at * wide : (at + 1) * wide]

    for layer in range(2):
        for group in range(width // 16):
            lanes = jnp.concatenate(
                [
                    raw[layer, :, pl.ds(16 * group + 8 * at, 8), :].reshape(8 * TAPS, wide)
                    for at in range(2)
                ],
                axis=1,
            )
            high, low = halves(lanes)
            mixed = (
                dot(mixers_ref[layer, 0], high)
                + dot(mixers_ref[layer, 0], low)
                + dot(mixers_ref[layer, 1], high)
            )
            rows = jnp.concatenate(
                [
                    mixed[:, at * wide : (at + 1) * wide].reshape(TAPS, 8, wide)
                    for at in range(2)
                ],
                axis=1,
            )
            out_ref[layer, :, pl.ds(16 * group, 16), :] = rows.astype(BF16)


def turned(block, axes, steps):
    sizes = [lax.axis_size(axis) for axis in axes]
    if not any(step % size for step, size in zip(steps, sizes)):
        return block
    route = []
    for place in np.ndindex(*sizes):
        target = [(at + step) % size for at, step, size in zip(place, steps, sizes)]
        route.append(
            (int(np.ravel_multi_index(place, sizes)), int(np.ravel_multi_index(target, sizes)))
        )
    return lax.ppermute(block, axes, route)


def shards(clip_input, first_kernel, second_kernel, out_grad, tap_mix, left_panels, right_panels):
    clips, frames, side, _, channels = clip_input.shape
    wide = first_kernel.shape[2]
    width = right_panels.shape[2]
    half, quarter = side // 2, side // 4
    half_frames = frames // 2
    cells = half_frames * half * half
    clip_parts = lax.axis_size("tm")
    cores, chips = lax.axis_size("core"), lax.axis_size("chip")
    equals = chips * clip_parts
    parts = equals * cores
    slices = lax.axis_size("fsdp")
    share = cells // slices
    assert clips == 1 and frames == 4
    x = clip_input.reshape(frames, half, 2, side, channels)
    grad = out_grad.reshape(quarter, quarter, channels)
    place, chip_at, core_at, half_at = (
        lax.axis_index(axis).reshape(1) for axis in ("fsdp", "chip", "core", "tm")
    )

    pick = jnp.asarray(column_picks(side), BF16)
    pad = (half // 8 + 1) * 8
    rows = quarter * quarter * channels // wide
    projected, halo = pl.pallas_call(
        project_kernel,
        out_shape=(
            jax.ShapeDtypeStruct((8 * cells + rows, wide), BF16),
            jax.ShapeDtypeStruct((half * half + rows, wide), F32),
        ),
        in_specs=[ANY] * 5,
        out_specs=(VMEM, VMEM),
        scratch_shapes=[
            pltpu.VMEM(x.shape, BF16),
            pltpu.VMEM(left_panels.shape[1:], F32),
            pltpu.VMEM(grad.shape, BF16),
            pltpu.VMEM(pick.shape, BF16),
            pltpu.VMEM((9,) + first_kernel.shape[1:], BF16),
            pltpu.VMEM((quarter * quarter, channels), F32),
            pltpu.VMEM((3, pad + half * half, wide), F32),
            pltpu.SemaphoreType.DMA((8,)),
        ],
        compiler_params=pltpu.CompilerParams(vmem_limit_bytes=58 << 20),
        cost_estimate=pl.CostEstimate(
            flops=4 * frames * side * side * channels * wide,
            bytes_accessed=PROJECT_COST,
            transcendentals=0,
        ),
    )(x, left_panels, grad, pick, first_kernel)
    if clip_parts == 2:
        prior = later = lax.ppermute(halo, "tm", [(0, 1), (1, 0)])
    else:
        prior, later = shifted(halo, "tm", 1), shifted(halo, "tm", -1)
    right = right_panels.transpose(0, 2, 1)
    right = [turned(right, ("fsdp",), (distance,)) for distance in range(slices)]
    projected, right = lax.optimization_barrier((projected, right))
    held = jnp.stack(
        [
            turned(projected, ("chip", "tm"), steps)
            for steps in np.ndindex(chips, clip_parts)
        ]
    )

    spread = jnp.asarray(spread_picks(half), BF16)
    acts = pl.pallas_call(
        functools.partial(hidden_kernel, clip_parts=clip_parts),
        out_shape=jax.ShapeDtypeStruct((equals, slices, 2, share, wide), BF16),
        in_specs=[SMEM] + [VMEM] * 6 + [HBM] * 2,
        out_specs=VMEM,
        scratch_shapes=[
            pltpu.VMEM((quarter * quarter, channels), F32),
            pltpu.VMEM((frames, 2, 2, half * half, channels), BF16),
            pltpu.VMEM(first_kernel.shape, BF16),
            pltpu.VMEM(second_kernel.shape, BF16),
            pltpu.VMEM((3, pad + cells, wide), F32),
            pltpu.SemaphoreType.DMA((2, 3)),
        ],
        compiler_params=pltpu.CompilerParams(vmem_limit_bytes=ROOM),
        cost_estimate=pl.CostEstimate(
            flops=3 * cells * TAPS * channels * wide,
            bytes_accessed=HIDDEN_COST,
            transcendentals=cells * wide,
        ),
    )(
        half_at, x, prior, grad, later, pick, spread, first_kernel, second_kernel,
    )
    acts, *right = lax.optimization_barrier((acts, *right))
    clip_cells = clip_parts * cells
    shift_picks, sort_picks, mixers = pl.pallas_call(
        functools.partial(tables_kernel, slices=slices, clip_parts=clip_parts, half=half),
        out_shape=(
            jax.ShapeDtypeStruct((clip_cells, 8 * clip_cells), BF16),
            jax.ShapeDtypeStruct((clip_cells, clip_cells), BF16),
            jax.ShapeDtypeStruct((2, 2, 8 * TAPS, 8 * TAPS), BF16),
        ),
        in_specs=[ANY, VMEM],
        out_specs=(VMEM,) * 3,
        compiler_params=pltpu.CompilerParams(vmem_limit_bytes=16 << 20),
        cost_estimate=pl.CostEstimate(flops=0, bytes_accessed=4 << 20, transcendentals=0),
    )(acts, tap_mix)
    every = lax.all_to_all(
        acts.reshape(equals * slices, 2, share, wide), ("chip", "tm", "fsdp"), 0, 0, tiled=True
    ).reshape(equals, slices, 2, share, wide)
    every, held = lax.optimization_barrier((every, held))
    every = [turned(every, ("core",), (cross,)) for cross in range(cores)]
    columns = pl.pallas_call(
        functools.partial(right_kernel, cores=cores),
        out_shape=jax.ShapeDtypeStruct((cores, 2 * width, equals * share), BF16),
        in_specs=[SMEM] * 2 + [VMEM] * (cores + slices),
        out_specs=VMEM,
        compiler_params=pltpu.CompilerParams(vmem_limit_bytes=16 << 20),
    )(place, core_at, *every, *right)
    columns, held = lax.optimization_barrier((columns, held))
    columns = [turned(columns, ("fsdp",), (distance,)) for distance in range(slices)]
    left_rows = [turned(held, ("core",), (cross,)) for cross in range(cores)]

    result = pl.pallas_call(
        functools.partial(
            update_kernel, slices=slices, cores=cores, clip_parts=clip_parts, half=half
        ),
        out_shape=jax.ShapeDtypeStruct((2, TAPS, width, wide), BF16),
        in_specs=[SMEM] * 4
        + [VMEM] * len(columns)
        + [ANY] * cores
        + [VMEM] * 4,
        out_specs=VMEM,
        scratch_shapes=[
            pltpu.VMEM((parts,) + projected.shape, BF16),
            pltpu.VMEM((slices, cores, 2 * width, equals * share), BF16),
            pltpu.VMEM((8, parts // clip_parts, width, clip_cells), BF16),
            pltpu.VMEM((parts * cells // 8 + (quarter + 1) * quarter + 8, wide), F32),
            pltpu.VMEM((2, TAPS, width, wide), F32),
            pltpu.SemaphoreType.DMA((parts,)),
        ],
        compiler_params=pltpu.CompilerParams(vmem_limit_bytes=40 << 20),
    )(
        place, chip_at, core_at, half_at,
        *columns, *left_rows, left_panels, mixers, shift_picks, sort_picks,
    )
    return result.transpose(0, 1, 3, 2)


def solution(mesh):
    fsdp, replica, tm = (mesh.shape[axis] for axis in ("fsdp", "replica", "tm"))
    cores = 2 if replica % 2 == 0 else 1
    assert mesh.axis_names == ("fsdp", "replica", "tm")
    mesh = Mesh(
        mesh.devices.reshape(fsdp, replica // cores, cores, tm), ("fsdp", "chip", "core", "tm")
    )
    replica = ("chip", "core")
    in_specs = (
        P(replica, "tm", None, None, None),
        P(None, None, "fsdp"),
        P(None, "fsdp", None),
        P(replica, "tm", None, None, None),
        P(),
        P(None, "fsdp", None),
        P(None, "fsdp", (*replica, "tm")),
    )
    out_specs = P(None, None, "fsdp", (*replica, "tm"))
    return jax.shard_map(shards, mesh=mesh, in_specs=in_specs, out_specs=out_specs, check_vma=False)
```

profile of v0, /device:TPU:0, one launch (start us, length us, event | category | flops | bytes accessed | tf_op | source)
XLA Modules:
  0.0 51.8 jit_solution(16539059400787398354)
XLA Ops:
  0.0 5.0 %collective-permute-start.3 = (f32[2,64,128]{2,1,0:T(8,128)}, f32[2,64,128]{2,1,0:T(8,128)S(1)}, u32[]{:S(2)}, u32[]{:S(2)}) collective-permute-start(f32[2,64,128]{2,1,0:T(8,128)} %bitcast.20), channel_id=1, source_target_pairs={{0,24},{8,0},{16,8},{24,16},{1,25},{9,1},{17,9},{25,17},{2,26},{10... | collective-permute-start | bytes 196616 | tf_op jit(solution)/shard_map/ppermute | solution.py:519
  5.0 0.0 collective-permute-start.2
  5.1 1.0 %collective-permute-start.1 = (f32[2,64,128]{2,1,0:T(8,128)}, f32[2,64,128]{2,1,0:T(8,128)S(1)}, u32[]{:S(2)}, u32[]{:S(2)}) collective-permute-start(f32[2,64,128]{2,1,0:T(8,128)} %bitcast.22), channel_id=1, source_target_pairs={{0,8},{8,16},{16,24},{24,0},{1,9},{9,17},{17,25},{25,1},{2,10},{10... | collective-permute-start | bytes 196616 | tf_op jit(solution)/shard_map/ppermute | solution.py:519
  6.1 4.3 %shard_map.91 = (bf16[1088,128]{1,0:T(8,128)(2,1)}, f32[128,128]{1,0:T(8,128)}) custom-call(bf16[4,8,2,16,512]{4,3,2,1,0:T(8,128)(2,1)} %bitcast.14, f32[2,128,512]{2,1,0:T(8,128)} %refs_6_.1, bf16[4,4,512]{2,1,0:T(4,128)(2,1)} %bitcast.18, bf16[128,128]{1,0:T(8,128)(2,1)} %constant.18.clone.pick_any.pick_ref, bf16[27,512,128]{2,1,0:T(8,128)(2,1)} %first_any.3), custom_call_target="tpu_custom_call" | custom-call | flops 268435456 | bytes 16777216 | tf_op jit(solution)/shard_map/pallas_call | solution.py:545
  10.4 1.6 %collective-permute-start = (f32[128,128]{1,0:T(8,128)}, f32[128,128]{1,0:T(8,128)S(1)}, u32[]{:S(2)}, u32[]{:S(2)}) collective-permute-start(f32[128,128]{1,0:T(8,128)} %get-tuple-element.24), channel_id=1, source_target_pairs={{0,1},{1,0},{2,3},{3,2},{4,5},{5,4},{6,7},{7,6},{8,9},{9,8},{10,11... | collective-permute-start | bytes 196616 | tf_op jit(solution)/shard_map/ppermute | solution.py:571
  11.9 0.0 collective-permute-done.3.refs_5_
  11.9 0.0 collective-permute-done.2.refs_4_
  12.0 0.0 collective-permute-done.1.refs_3_
  12.0 2.2 %collective-permute-start.6 = (bf16[1088,128]{1,0:T(8,128)(2,1)}, bf16[1088,128]{1,0:T(8,128)(2,1)S(1)}, u32[]{:S(2)}, u32[]{:S(2)}) collective-permute-start(bf16[1088,128]{1,0:T(8,128)(2,1)} %get-tuple-element.31), channel_id=1, source_target_pairs={{0,5},{1,4},{4,1},{5,0},{2,7},{3,6},{6,3},{7,2},{8,13},{9,12},{12,... | collective-permute-start | bytes 835592 | tf_op jit(solution)/shard_map/ppermute | solution.py:519
  14.2 0.5 collective-permute-start.5
  14.7 0.8 %collective-permute-start.4 = (bf16[1088,128]{1,0:T(8,128)(2,1)}, bf16[1088,128]{1,0:T(8,128)(2,1)S(1)}, u32[]{:S(2)}, u32[]{:S(2)}) collective-permute-start(bf16[1088,128]{1,0:T(8,128)(2,1)} %get-tuple-element.31), channel_id=1, source_target_pairs={{0,1},{1,0},{4,5},{5,4},{2,3},{3,2},{6,7},{7,6},{8,9},{9,8},{12,13... | collective-permute-start | bytes 835592 | tf_op jit(solution)/shard_map/ppermute | solution.py:519
  15.5 0.0 collective-permute-done.prior_ref.later_ref
  15.6 5.4 %shard_map.92.after_any = bf16[4,4,2,32,128]{4,3,2,1,0:T(8,128)(2,1)} custom-call(s32[1]{0:T(128)} %bitcast.3.tm_ref, bf16[4,8,2,16,512]{4,3,2,1,0:T(8,128)(2,1)S(1)} %bitcast.15, f32[128,128]{1,0:T(8,128)S(1)} %collective-permute-done.prior_ref.later_ref, bf16[4,4,512]{2,1,0:T(4,128)(2,1)S(1)} %bitcast.19, ...), custom_call_target="tpu_custom_call" | custom-call | flops 679477248 | bytes 209715200 | tf_op jit(solution)/shard_map/pallas_call | solution.py:585
  21.0 6.3 %all-to-all-start = ((bf16[16,2,32,128]{3,2,1,0:T(8,128)(2,1)}), bf16[16,2,32,128]{3,2,1,0:T(8,128)(2,1)S(1)}, u32[]{:S(2)}, u32[]{:S(2)}) async-start(bf16[16,2,32,128]{3,2,1,0:T(8,128)(2,1)} %bitcast.7), calls=%async_computation | async-start | bytes 524288 | tf_op jit(solution)/shard_map/all_to_all | solution.py:621
  27.3 0.0 collective-permute-done.6
  27.3 0.6 %collective-permute-done.5 = bf16[1088,128]{1,0:T(8,128)(2,1)S(1)} collective-permute-done((bf16[1088,128]{1,0:T(8,128)(2,1)}, bf16[1088,128]{1,0:T(8,128)(2,1)S(1)}, u32[]{:S(2)}, u32[]{:S(2)}) %collective-permute-start.5) | collective-permute-done | bytes 278560 | tf_op jit(solution)/shard_map/ppermute | solution.py:519
  27.9 0.0 collective-permute-done.4
  27.9 0.0 copy-start.7
  27.9 0.1 pad_maximum_fusion.refs_4_
  28.1 0.0 copy-start.1
  28.1 8.0 %all-to-all-done = bf16[16,2,32,128]{3,2,1,0:T(8,128)(2,1)S(1)} async-done(((bf16[16,2,32,128]{3,2,1,0:T(8,128)(2,1)}), bf16[16,2,32,128]{3,2,1,0:T(8,128)(2,1)S(1)}, u32[]{:S(2)}, u32[]{:S(2)}) %all-to-all-start) | async-done | bytes 262176 | tf_op jit(solution)/shard_map/all_to_all | solution.py:621
  36.1 1.5 %collective-permute-done.7.refs_1_ = bf16[4,4,2,32,128]{4,3,2,1,0:T(8,128)(2,1)S(1)} collective-permute-done((bf16[4,4,2,32,128]{4,3,2,1,0:T(8,128)(2,1)S(1)}, bf16[4,4,2,32,128]{4,3,2,1,0:T(8,128)(2,1)S(1)}, u32[]{:S(2)}, u32[]{:S(2)}) %collective-permute-start.7) | collective-permute-done | bytes 262176 | tf_op jit(solution)/shard_map/ppermute | solution.py:519
  37.6 0.5 shard_map.93.refs_0_
  38.1 0.2 collective-permute-start.11
  38.3 0.3 collective-permute-start.10
  38.6 2.2 %collective-permute-start.9 = (bf16[2,128,128]{2,1,0:T(8,128)(2,1)S(1)}, bf16[2,128,128]{2,1,0:T(8,128)(2,1)S(1)}, u32[]{:S(2)}, u32[]{:S(2)}) collective-permute-start(bf16[2,128,128]{2,1,0:T(8,128)(2,1)S(1)} %shard_map.93.refs_0_), channel_id=1, source_target_pairs={{0,16},{8,24},{16,0},{24,8},{1,17},{9,25},{17,1},{25,9},{2,18},{10... | collective-permute-start | bytes 196616 | tf_op jit(solution)/shard_map/ppermute | solution.py:519
  40.9 0.0 collective-permute-start.8
  40.9 0.9 %shard_map.94 = (bf16[256,2048]{1,0:T(8,128)(2,1)S(1)}, bf16[256,256]{1,0:T(8,128)(2,1)S(1)}, bf16[2,2,216,216]{3,2,1,0:T(8,128)(2,1)S(1)}) custom-call(bf16[4,4,2,32,128]{4,3,2,1,0:T(8,128)(2,1)} %shard_map.92.after_any, f32[2,27,27]{2,1,0:T(8,128)S(1)} %copy.10.mix_ref), custom_call_target="tpu_custom_call" | custom-call | bytes 4194304 | tf_op jit(solution)/shard_map/pallas_call | solution.py:609
  41.8 0.9 %collective-permute-done.10.refs_3_ = bf16[2,128,128]{2,1,0:T(8,128)(2,1)S(1)} collective-permute-done((bf16[2,128,128]{2,1,0:T(8,128)(2,1)S(1)}, bf16[2,128,128]{2,1,0:T(8,128)(2,1)S(1)}, u32[]{:S(2)}, u32[]{:S(2)}) %collective-permute-start.10) | collective-permute-done | bytes 65568 | tf_op jit(solution)/shard_map/ppermute | solution.py:519
  42.7 4.8 %collective-permute-done.9.refs_2_ = bf16[2,128,128]{2,1,0:T(8,128)(2,1)S(1)} collective-permute-done((bf16[2,128,128]{2,1,0:T(8,128)(2,1)S(1)}, bf16[2,128,128]{2,1,0:T(8,128)(2,1)S(1)}, u32[]{:S(2)}, u32[]{:S(2)}) %collective-permute-start.9) | collective-permute-done | bytes 65568 | tf_op jit(solution)/shard_map/ppermute | solution.py:519
  47.4 0.0 collective-permute-done.11.refs_5_
  47.4 4.3 %shard_map.95 = bf16[2,27,64,128]{3,2,1,0:T(8,128)(2,1)} custom-call(s32[1]{0:T(128)} %bitcast.place_ref, s32[1]{0:T(128)} %bitcast.1.chip_ref, s32[1]{0:T(128)} %bitcast.2.core_ref, s32[1]{0:T(128)} %bitcast.3.tm_ref, bf16[2,128,128]{2,1,0:T(8,128)(2,1)S(1)} %shard_map.93.refs_0_, bf16[2,128,128]{2,1,0:T(8,128)(2,1)S(1)} %collective-permute-done.8.refs_1_, ...), custom_call_target="tpu_custom_call" | custom-call | tf_op jit(solution)/shard_map/pallas_call | solution.py:637
  (17 shorter events, 0.0 us)
Async XLA Ops:
  0.0 11.9 %collective-permute-start.3 = (f32[2,64,128]{2,1,0:T(8,128)}, f32[2,64,128]{2,1,0:T(8,128)S(1)}, u32[]{:S(2)}, u32[]{:S(2)}) collective-permute-start(f32[2,64,128]{2,1,0:T(8,128)} %bitcast.20), channel_id=1, source_target_pairs={{0,24},{8,0},{16,8},{24,16},{1,25},{9,1},{17,9},{25,17},{2,26},{10... | collective-permute-start | bytes 196616 | tf_op jit(solution)/shard_map/ppermute | solution.py:519
  5.0 6.9 %collective-permute-start.2 = (f32[2,64,128]{2,1,0:T(8,128)}, f32[2,64,128]{2,1,0:T(8,128)S(1)}, u32[]{:S(2)}, u32[]{:S(2)}) collective-permute-start(f32[2,64,128]{2,1,0:T(8,128)} %bitcast.21), channel_id=1, source_target_pairs={{0,16},{8,24},{16,0},{24,8},{1,17},{9,25},{17,1},{25,9},{2,18},{10... | collective-permute-start | bytes 196616 | tf_op jit(solution)/shard_map/ppermute | solution.py:519
  5.1 6.9 %collective-permute-start.1 = (f32[2,64,128]{2,1,0:T(8,128)}, f32[2,64,128]{2,1,0:T(8,128)S(1)}, u32[]{:S(2)}, u32[]{:S(2)}) collective-permute-start(f32[2,64,128]{2,1,0:T(8,128)} %bitcast.22), channel_id=1, source_target_pairs={{0,8},{8,16},{16,24},{24,0},{1,9},{9,17},{17,25},{25,1},{2,10},{10... | collective-permute-start | bytes 196616 | tf_op jit(solution)/shard_map/ppermute | solution.py:519
  6.1 9.5 %copy-start = (bf16[1,4,16,16,512]{4,3,2,1,0:T(8,128)(2,1)S(1)}, bf16[1,4,16,16,512]{4,3,2,1,0:T(8,128)(2,1)}, u32[]{:S(2)}) copy-start(bf16[1,4,16,16,512]{4,3,2,1,0:T(8,128)(2,1)} %param.9) | copy-start | bytes 3145732
  6.1 9.5 %copy-start.2 = (bf16[576,16]{1,0:T(8,128)(2,1)S(1)}, bf16[576,16]{1,0:T(8,128)(2,1)}, u32[]{:S(2)}) copy-start(bf16[576,16]{1,0:T(8,128)(2,1)} %constant.19.clone.spread_ref) | copy-start | bytes 55300
  6.1 9.5 %copy-start.3 = (bf16[128,128]{1,0:T(8,128)(2,1)S(1)}, bf16[128,128]{1,0:T(8,128)(2,1)}, u32[]{:S(2)}) copy-start(bf16[128,128]{1,0:T(8,128)(2,1)} %constant.18.clone.pick_any.pick_ref) | copy-start | bytes 98308
  6.1 9.5 %copy-start.4 = (bf16[1,1,4,4,512]{4,3,2,1,0:T(4,128)(2,1)S(1)}, bf16[1,1,4,4,512]{4,3,2,1,0:T(4,128)(2,1)}, u32[]{:S(2)}) copy-start(bf16[1,1,4,4,512]{4,3,2,1,0:T(4,128)(2,1)} %param.12) | copy-start | bytes 49156
  10.4 5.1 %collective-permute-start = (f32[128,128]{1,0:T(8,128)}, f32[128,128]{1,0:T(8,128)S(1)}, u32[]{:S(2)}, u32[]{:S(2)}) collective-permute-start(f32[128,128]{1,0:T(8,128)} %get-tuple-element.24), channel_id=1, source_target_pairs={{0,1},{1,0},{2,3},{3,2},{4,5},{5,4},{6,7},{7,6},{8,9},{9,8},{10,11... | collective-permute-start | bytes 196616 | tf_op jit(solution)/shard_map/ppermute | solution.py:571
  12.0 15.3 %collective-permute-start.6 = (bf16[1088,128]{1,0:T(8,128)(2,1)}, bf16[1088,128]{1,0:T(8,128)(2,1)S(1)}, u32[]{:S(2)}, u32[]{:S(2)}) collective-permute-start(bf16[1088,128]{1,0:T(8,128)(2,1)} %get-tuple-element.31), channel_id=1, source_target_pairs={{0,5},{1,4},{4,1},{5,0},{2,7},{3,6},{6,3},{7,2},{8,13},{9,12},{12,... | collective-permute-start | bytes 835592 | tf_op jit(solution)/shard_map/ppermute | solution.py:519
  14.2 13.7 %collective-permute-start.5 = (bf16[1088,128]{1,0:T(8,128)(2,1)}, bf16[1088,128]{1,0:T(8,128)(2,1)S(1)}, u32[]{:S(2)}, u32[]{:S(2)}) collective-permute-start(bf16[1088,128]{1,0:T(8,128)(2,1)} %get-tuple-element.31), channel_id=1, source_target_pairs={{0,4},{1,5},{4,0},{5,1},{2,6},{3,7},{6,2},{7,3},{8,12},{9,13},{12,... | collective-permute-start | bytes 835592 | tf_op jit(solution)/shard_map/ppermute | solution.py:519
  14.7 13.2 %collective-permute-start.4 = (bf16[1088,128]{1,0:T(8,128)(2,1)}, bf16[1088,128]{1,0:T(8,128)(2,1)S(1)}, u32[]{:S(2)}, u32[]{:S(2)}) collective-permute-start(bf16[1088,128]{1,0:T(8,128)(2,1)} %get-tuple-element.31), channel_id=1, source_target_pairs={{0,1},{1,0},{4,5},{5,4},{2,3},{3,2},{6,7},{7,6},{8,9},{9,8},{12,13... | collective-permute-start | bytes 835592 | tf_op jit(solution)/shard_map/ppermute | solution.py:519
  15.5 12.4 %copy-start.6 = (bf16[1088,128]{1,0:T(8,128)(2,1)S(1)}, bf16[1088,128]{1,0:T(8,128)(2,1)}, u32[]{:S(2)}) copy-start(bf16[1088,128]{1,0:T(8,128)(2,1)} %get-tuple-element.31) | copy-start | bytes 835588
  21.0 15.1 %all-to-all-start = ((bf16[16,2,32,128]{3,2,1,0:T(8,128)(2,1)}), bf16[16,2,32,128]{3,2,1,0:T(8,128)(2,1)S(1)}, u32[]{:S(2)}, u32[]{:S(2)}) async-start(bf16[16,2,32,128]{3,2,1,0:T(8,128)(2,1)} %bitcast.7), calls=%async_computation | async-start | bytes 524288 | tf_op jit(solution)/shard_map/all_to_all | solution.py:621
  27.9 9.7 %copy-start.5 = (f32[2,128,64]{1,2,0:T(8,128)S(1)}, f32[2,128,64]{1,2,0:T(8,128)}, u32[]{:S(2)}) copy-start(f32[2,128,64]{1,2,0:T(8,128)} %param.15) | copy-start | bytes 196612
  27.9 13.0 %copy-start.7 = (f32[2,27,27]{2,0,1:T(2,128)S(1)}, f32[2,27,27]{2,0,1:T(2,128)}, u32[]{:S(2)}) copy-start(f32[2,27,27]{2,0,1:T(2,128)} %param.13) | copy-start | bytes 17500
  28.1 19.3 %copy-start.1 = (f32[2,128,512]{2,1,0:T(8,128)S(1)}, f32[2,128,512]{2,1,0:T(8,128)}, u32[]{:S(2)}) copy-start(f32[2,128,512]{2,1,0:T(8,128)} %refs_6_.1) | copy-start | bytes 1572868
  36.1 1.5 %collective-permute-start.7 = (bf16[4,4,2,32,128]{4,3,2,1,0:T(8,128)(2,1)S(1)}, bf16[4,4,2,32,128]{4,3,2,1,0:T(8,128)(2,1)S(1)}, u32[]{:S(2)}, u32[]{:S(2)}) collective-permute-start(bf16[4,4,2,32,128]{4,3,2,1,0:T(8,128)(2,1)S(1)} %bitcast.16), channel_id=1, source_target_pairs={{0,2},{2,0},{1,3},{3,1},{4,6},{6,4},{5,7},{7,5},{8,10},{10,8},{9,1... | collective-permute-start | bytes 786440 | tf_op jit(solution)/shard_map/ppermute | solution.py:519
  38.1 9.3 %collective-permute-start.11 = (bf16[4,1088,128]{2,1,0:T(8,128)(2,1)S(1)}, bf16[4,1088,128]{2,1,0:T(8,128)(2,1)S(1)}, u32[]{:S(2)}, u32[]{:S(2)}) collective-permute-start(bf16[4,1088,128]{2,1,0:T(8,128)(2,1)S(1)} %pad_maximum_fusion.refs_4_), channel_id=1, source_target_pairs={{0,2},{2,0},{1,3},{3,1},{4,6},{6,4},{5,7},{7,5},{8,10},{10,8},{9,1... | collective-permute-start | bytes 3342344 | tf_op jit(solution)/shard_map/ppermute | solution.py:519
  38.3 4.4 %collective-permute-start.10 = (bf16[2,128,128]{2,1,0:T(8,128)(2,1)S(1)}, bf16[2,128,128]{2,1,0:T(8,128)(2,1)S(1)}, u32[]{:S(2)}, u32[]{:S(2)}) collective-permute-start(bf16[2,128,128]{2,1,0:T(8,128)(2,1)S(1)} %shard_map.93.refs_0_), channel_id=1, source_target_pairs={{0,24},{8,0},{16,8},{24,16},{1,25},{9,1},{17,9},{25,17},{2,26},{10... | collective-permute-start | bytes 196616 | tf_op jit(solution)/shard_map/ppermute | solution.py:519
  38.6 8.8 %collective-permute-start.9 = (bf16[2,128,128]{2,1,0:T(8,128)(2,1)S(1)}, bf16[2,128,128]{2,1,0:T(8,128)(2,1)S(1)}, u32[]{:S(2)}, u32[]{:S(2)}) collective-permute-start(bf16[2,128,128]{2,1,0:T(8,128)(2,1)S(1)} %shard_map.93.refs_0_), channel_id=1, source_target_pairs={{0,16},{8,24},{16,0},{24,8},{1,17},{9,25},{17,1},{25,9},{2,18},{10... | collective-permute-start | bytes 196616 | tf_op jit(solution)/shard_map/ppermute | solution.py:519
  40.9 6.5 %collective-permute-start.8 = (bf16[2,128,128]{2,1,0:T(8,128)(2,1)S(1)}, bf16[2,128,128]{2,1,0:T(8,128)(2,1)S(1)}, u32[]{:S(2)}, u32[]{:S(2)}) collective-permute-start(bf16[2,128,128]{2,1,0:T(8,128)(2,1)S(1)} %shard_map.93.refs_0_), channel_id=1, source_target_pairs={{0,8},{8,16},{16,24},{24,0},{1,9},{9,17},{17,25},{25,1},{2,10},{10... | collective-permute-start | bytes 196616 | tf_op jit(solution)/shard_map/ppermute | solution.py:519
where the time goes:
time: 52 us; the launch traced here: 51.8 us
  starting transfers between devices  20.2 us (39%)
  waiting for transfers between devices  15.8 us (30%)
  Pallas kernels  15.4 us (30%)
    ppermute x11, starting transfers between devices, turned(): return lax.ppermute(block, axes, route)  12.4 us
    all_to_all x1, waiting for transfers between devices, shards(): lax.all_to_all(acts.reshape(equals * slices, 2, share, wide), ('chip', 't...  8 us
    ppermute x11, waiting for transfers between devices, turned(): return lax.ppermute(block, axes, route)  7.8 us
    all_to_all x1, starting transfers between devices, shards(): lax.all_to_all(acts.reshape(equals * slices, 2, share, wide), ('chip', 't...  6.26 us
    pallas_call x1, Pallas kernels, shards(): pl.pallas_call(functools.partial(hidden_kernel, clip_parts=clip_parts), o...  5.44 us
    pallas_call x1, Pallas kernels, shards(): pl.pallas_call(functools.partial(update_kernel, slices=slices, cores=core...  4.33 us
    pallas_call x1, Pallas kernels, shards(): pl.pallas_call(project_kernel, out_shape=(jax.ShapeDtypeStruct((8 * cells...  4.31 us
    ppermute x1, starting transfers between devices, shards(): prior = later = lax.ppermute(halo, 'tm', [(0, 1), (1, 0)])  1.56 us
  transfers between devices with their start and end apart: 13, of which 5 were waited for; matrix products, arithmetic and copies ran while one was open for 0% of the time, Pallas kernels for 21%

commit v1 on v0

--- a/solution.py
+++ b/solution.py
@@ -275,13 +275,17 @@
 def right_kernel(place_ref, core_ref, *refs, cores):
     acts_refs, right_refs, out_ref = refs[:cores], refs[cores:-1], refs[-1]
     parts, slices = acts_refs[0].shape[:2]
-    width = right_refs[0].shape[1]
+    width = right_refs[0].shape[2]
     for layer in range(2):
-        rights = [jnp.concatenate(halves(ref[layer]), axis=0) for ref in right_refs]
+        rights = [
+            jnp.concatenate(halves(ref[at, layer]), axis=0)
+            for ref in right_refs
+            for at in range(ref.shape[0])
+        ]
         for cross, acts_ref in enumerate(acts_refs):
             total = None
             for distance in range(slices):
-                origin = lax.rem(place_ref[0] + (slices - distance), slices)
+                origin = factor_origin(place_ref[0], distance, slices)
                 rows = jnp.concatenate(
                     [acts_ref[part, origin, layer] for part in range(parts)], axis=0
                 )
@@ -517,6 +521,36 @@
             (int(np.ravel_multi_index(place, sizes)), int(np.ravel_multi_index(target, sizes)))
         )
     return lax.ppermute(block, axes, route)
+
+
+def doubled(size):
+    return size & (size - 1) == 0
+
+
+def first_round(block):
+    size = lax.axis_size("fsdp")
+    if not doubled(size):
+        return [block] + [turned(block, ("fsdp",), (distance,)) for distance in range(1, size)]
+    if size == 1:
+        return [block]
+    return [block, lax.ppermute(block, "fsdp", [(i, i ^ 1) for i in range(size)])]
+
+
+def later_rounds(blocks):
+    size = lax.axis_size("fsdp")
+    held = [block[None] for block in blocks]
+    step = 2
+    while doubled(size) and step < size:
+        route = [(i, i ^ step) for i in range(size)]
+        held.append(lax.ppermute(jnp.concatenate(held, axis=0), "fsdp", route))
+        step *= 2
+    return held
+
+
+def factor_origin(place, distance, size):
+    if doubled(size):
+        return place ^ distance
+    return lax.rem(place + (size - distance), size)
 
 
 def shards(clip_input, first_kernel, second_kernel, out_grad, tap_mix, left_panels, right_panels):
@@ -572,8 +606,9 @@
     else:
         prior, later = shifted(halo, "tm", 1), shifted(halo, "tm", -1)
     right = right_panels.transpose(0, 2, 1)
-    right = [turned(right, ("fsdp",), (distance,)) for distance in range(slices)]
+    right = first_round(right)
     projected, right = lax.optimization_barrier((projected, right))
+    right = later_rounds(right)
     held = jnp.stack(
         [
             turned(projected, ("chip", "tm"), steps)
@@ -626,7 +661,7 @@
     columns = pl.pallas_call(
         functools.partial(right_kernel, cores=cores),
         out_shape=jax.ShapeDtypeStruct((cores, 2 * width, equals * share), BF16),
-        in_specs=[SMEM] * 2 + [VMEM] * (cores + slices),
+        in_specs=[SMEM] * 2 + [VMEM] * (cores + len(right)),
         out_specs=VMEM,
         compiler_params=pltpu.CompilerParams(vmem_limit_bytes=16 << 20),
     )(place, core_at, *every, *right)

time: 52 us -> 49.4 us (0.950)
  starting transfers between devices: 20.2 us -> 17.5 us
    ppermute x11 -> x8, starting transfers between devices: 12.4 us -> 6.27 us  [turned(): return lax.ppermute(block, axes, route)]
    ppermute x0 -> x2, starting transfers between devices: none -> 5.67 us  [the longest x1 3.02 us: first_round(): lax.ppermute(block, 'fsdp', [(i, i ^ 1) for i in range(size)])]
    all_to_all x1, starting transfers between devices: 6.26 us -> 4.09 us  [shards(): lax.all_to_all(acts.reshape(equals * slices, 2, share, wide), ('chip', 't...]
    ppermute x11 -> x8, waiting for transfers between devices: 7.8 us -> 9.85 us  [turned(): return lax.ppermute(block, axes, route)]
    all_to_all x1, waiting for transfers between devices: 8 us -> 5.96 us  [shards(): lax.all_to_all(acts.reshape(equals * slices, 2, share, wide), ('chip', 't...]
  transfers between devices with their start and end apart: 13 -> 12, of which waited for: 5 -> 6; matrix products, arithmetic and copies ran while one was open for 0% -> 0% of each run, Pallas kernels for 21% -> 22%
where the time goes in v1:
time: 49.4 us; the launch traced here: 49.1 us
  starting transfers between devices  17.5 us (35%)
  waiting for transfers between devices  15.8 us (32%)
  Pallas kernels  15.4 us (31%)
    ppermute x8, waiting for transfers between devices, turned(): return lax.ppermute(block, axes, route)  9.85 us
    ppermute x8, starting transfers between devices, turned(): return lax.ppermute(block, axes, route)  6.27 us
    all_to_all x1, waiting for transfers between devices, shards(): lax.all_to_all(acts.reshape(equals * slices, 2, share, wide), ('chip', 't...  5.96 us
    pallas_call x1, Pallas kernels, shards(): pl.pallas_call(functools.partial(hidden_kernel, clip_parts=clip_parts), o...  5.44 us
    pallas_call x1, Pallas kernels, shards(): pl.pallas_call(functools.partial(update_kernel, slices=slices, cores=core...  4.33 us
    pallas_call x1, Pallas kernels, shards(): pl.pallas_call(project_kernel, out_shape=(jax.ShapeDtypeStruct((8 * cells...  4.31 us
    all_to_all x1, starting transfers between devices, shards(): lax.all_to_all(acts.reshape(equals * slices, 2, share, wide), ('chip', 't...  4.09 us
    ppermute x1, starting transfers between devices, first_round(): lax.ppermute(block, 'fsdp', [(i, i ^ 1) for i in range(size)])  3.02 us
  transfers between devices with their start and end apart: 12, of which 6 were waited for; matrix products, arithmetic and copies ran while one was open for 0% of the time, Pallas kernels for 22%

profile of v1, /device:TPU:0, one launch (start us, length us, event | category | flops | bytes accessed | tf_op | source)
XLA Modules:
  0.0 49.1 jit_solution(15594311648758596287)
XLA Ops:
  0.0 3.0 %collective-permute-start.1 = (f32[2,64,128]{2,1,0:T(8,128)}, f32[2,64,128]{2,1,0:T(8,128)S(1)}, u32[]{:S(2)}, u32[]{:S(2)}) collective-permute-start(f32[2,64,128]{2,1,0:T(8,128)} %bitcast.20), channel_id=1, source_target_pairs={{0,8},{8,0},{16,24},{24,16},{1,9},{9,1},{17,25},{25,17},{2,10},{10... | collective-permute-start | bytes 196616 | tf_op jit(solution)/shard_map/ppermute | solution.py:536
  3.0 0.0 copy-start.5
  3.0 4.3 %shard_map.91 = (bf16[1088,128]{1,0:T(8,128)(2,1)}, f32[128,128]{1,0:T(8,128)}) custom-call(bf16[4,8,2,16,512]{4,3,2,1,0:T(8,128)(2,1)} %bitcast.16, f32[2,128,512]{2,1,0:T(8,128)} %refs_6_.1, bf16[4,4,512]{2,1,0:T(4,128)(2,1)} %bitcast.25, bf16[128,128]{1,0:T(8,128)(2,1)} %constant.18.clone.pick_any.pick_ref, bf16[27,512,128]{2,1,0:T(8,128)(2,1)} %first_any.3), custom_call_target="tpu_custom_call" | custom-call | flops 268435456 | bytes 16777216 | tf_op jit(solution)/shard_map/pallas_call | solution.py:579
  7.4 0.0 collective-permute-done.1
  7.4 2.7 %collective-permute-start.2 = (f32[2,2,64,128]{3,2,1,0:T(8,128)S(1)}, f32[2,2,64,128]{3,2,1,0:T(8,128)S(1)}, u32[]{:S(2)}, u32[]{:S(2)}) collective-permute-start(f32[2,2,64,128]{3,2,1,0:T(8,128)S(1)} %pad_maximum_fusion.1), channel_id=1, source_target_pairs={{0,16},{8,24},{16,0},{24,8},{1,17},{9,25},{17,1},{25,9},{2,18},{10... | collective-permute-start | bytes 393224 | tf_op jit(solution)/shard_map/ppermute | solution.py:545
  10.1 1.5 %collective-permute-start = (f32[128,128]{1,0:T(8,128)}, f32[128,128]{1,0:T(8,128)S(1)}, u32[]{:S(2)}, u32[]{:S(2)}) collective-permute-start(f32[128,128]{1,0:T(8,128)} %get-tuple-element.21), channel_id=1, source_target_pairs={{0,1},{1,0},{2,3},{3,2},{4,5},{5,4},{6,7},{7,6},{8,9},{9,8},{10,11... | collective-permute-start | bytes 196616 | tf_op jit(solution)/shard_map/ppermute | solution.py:605
  11.6 1.5 %collective-permute-start.5 = (bf16[1088,128]{1,0:T(8,128)(2,1)}, bf16[1088,128]{1,0:T(8,128)(2,1)S(1)}, u32[]{:S(2)}, u32[]{:S(2)}) collective-permute-start(bf16[1088,128]{1,0:T(8,128)(2,1)} %get-tuple-element.26), channel_id=1, source_target_pairs={{0,5},{1,4},{4,1},{5,0},{2,7},{3,6},{6,3},{7,2},{8,13},{9,12},{12,... | collective-permute-start | bytes 835592 | tf_op jit(solution)/shard_map/ppermute | solution.py:523
  13.0 0.5 %collective-permute-start.4 = (bf16[1088,128]{1,0:T(8,128)(2,1)}, bf16[1088,128]{1,0:T(8,128)(2,1)S(1)}, u32[]{:S(2)}, u32[]{:S(2)}) collective-permute-start(bf16[1088,128]{1,0:T(8,128)(2,1)} %get-tuple-element.26), channel_id=1, source_target_pairs={{0,4},{1,5},{4,0},{5,1},{2,6},{3,7},{6,2},{7,3},{8,12},{9,13},{12,... | collective-permute-start | bytes 835592 | tf_op jit(solution)/shard_map/ppermute | solution.py:523
  13.5 1.5 %collective-permute-start.3 = (bf16[1088,128]{1,0:T(8,128)(2,1)}, bf16[1088,128]{1,0:T(8,128)(2,1)S(1)}, u32[]{:S(2)}, u32[]{:S(2)}) collective-permute-start(bf16[1088,128]{1,0:T(8,128)(2,1)} %get-tuple-element.26), channel_id=1, source_target_pairs={{0,1},{1,0},{4,5},{5,4},{2,3},{3,2},{6,7},{7,6},{8,9},{9,8},{12,13... | collective-permute-start | bytes 835592 | tf_op jit(solution)/shard_map/ppermute | solution.py:523
  15.0 0.0 collective-permute-done.prior_ref.later_ref
  15.1 5.4 %shard_map.92.after_any = bf16[4,4,2,32,128]{4,3,2,1,0:T(8,128)(2,1)} custom-call(s32[1]{0:T(128)} %bitcast.3.tm_ref, bf16[4,8,2,16,512]{4,3,2,1,0:T(8,128)(2,1)S(1)} %bitcast.17, f32[128,128]{1,0:T(8,128)S(1)} %collective-permute-done.prior_ref.later_ref, bf16[4,4,512]{2,1,0:T(4,128)(2,1)S(1)} %bitcast.26, ...), custom_call_target="tpu_custom_call" | custom-call | flops 679477248 | bytes 209715200 | tf_op jit(solution)/shard_map/pallas_call | solution.py:620
  20.5 0.0 collective-permute-done.2.refs_4_
  20.5 4.1 %all-to-all-start = ((bf16[16,2,32,128]{3,2,1,0:T(8,128)(2,1)}), bf16[16,2,32,128]{3,2,1,0:T(8,128)(2,1)S(1)}, u32[]{:S(2)}, u32[]{:S(2)}) async-start(bf16[16,2,32,128]{3,2,1,0:T(8,128)(2,1)} %bitcast.9), calls=%async_computation | async-start | bytes 524288 | tf_op jit(solution)/shard_map/all_to_all | solution.py:656
  24.6 0.0 collective-permute-done.5
  24.6 2.4 %collective-permute-done.4 = bf16[1088,128]{1,0:T(8,128)(2,1)S(1)} collective-permute-done((bf16[1088,128]{1,0:T(8,128)(2,1)}, bf16[1088,128]{1,0:T(8,128)(2,1)S(1)}, u32[]{:S(2)}, u32[]{:S(2)}) %collective-permute-start.4) | collective-permute-done | bytes 278560 | tf_op jit(solution)/shard_map/ppermute | solution.py:523
  27.1 0.3 collective-permute-done.3
  27.4 0.1 pad_maximum_fusion.refs_4_
  27.5 0.0 copy-start.1
  27.5 6.0 %all-to-all-done = bf16[16,2,32,128]{3,2,1,0:T(8,128)(2,1)S(1)} async-done(((bf16[16,2,32,128]{3,2,1,0:T(8,128)(2,1)}), bf16[16,2,32,128]{3,2,1,0:T(8,128)(2,1)S(1)}, u32[]{:S(2)}, u32[]{:S(2)}) %all-to-all-start) | async-done | bytes 262176 | tf_op jit(solution)/shard_map/all_to_all | solution.py:656
  33.5 0.0 collective-permute-start.6
  33.5 1.5 %collective-permute-done.6.refs_1_ = bf16[4,4,2,32,128]{4,3,2,1,0:T(8,128)(2,1)S(1)} collective-permute-done((bf16[4,4,2,32,128]{4,3,2,1,0:T(8,128)(2,1)S(1)}, bf16[4,4,2,32,128]{4,3,2,1,0:T(8,128)(2,1)S(1)}, u32[]{:S(2)}, u32[]{:S(2)}) %collective-permute-start.6) | collective-permute-done | bytes 262176 | tf_op jit(solution)/shard_map/ppermute | solution.py:523
  35.0 0.5 shard_map.93.refs_0_
  35.5 0.2 collective-permute-start.10
  35.7 0.3 collective-permute-start.9
  36.0 2.2 %collective-permute-start.8 = (bf16[2,128,128]{2,1,0:T(8,128)(2,1)S(1)}, bf16[2,128,128]{2,1,0:T(8,128)(2,1)S(1)}, u32[]{:S(2)}, u32[]{:S(2)}) collective-permute-start(bf16[2,128,128]{2,1,0:T(8,128)(2,1)S(1)} %shard_map.93.refs_0_), channel_id=1, source_target_pairs={{0,16},{8,24},{16,0},{24,8},{1,17},{9,25},{17,1},{25,9},{2,18},{10... | collective-permute-start | bytes 196616 | tf_op jit(solution)/shard_map/ppermute | solution.py:523
  38.2 0.0 collective-permute-start.7
  38.3 0.9 %shard_map.94 = (bf16[256,2048]{1,0:T(8,128)(2,1)S(1)}, bf16[256,256]{1,0:T(8,128)(2,1)S(1)}, bf16[2,2,216,216]{3,2,1,0:T(8,128)(2,1)S(1)}) custom-call(bf16[4,4,2,32,128]{4,3,2,1,0:T(8,128)(2,1)} %shard_map.92.after_any, f32[2,27,27]{2,1,0:T(8,128)S(1)} %copy.10.mix_ref), custom_call_target="tpu_custom_call" | custom-call | bytes 4194304 | tf_op jit(solution)/shard_map/pallas_call | solution.py:644
  39.2 0.9 %collective-permute-done.9.refs_3_ = bf16[2,128,128]{2,1,0:T(8,128)(2,1)S(1)} collective-permute-done((bf16[2,128,128]{2,1,0:T(8,128)(2,1)S(1)}, bf16[2,128,128]{2,1,0:T(8,128)(2,1)S(1)}, u32[]{:S(2)}, u32[]{:S(2)}) %collective-permute-start.9) | collective-permute-done | bytes 65568 | tf_op jit(solution)/shard_map/ppermute | solution.py:523
  40.0 4.8 %collective-permute-done.8.refs_2_ = bf16[2,128,128]{2,1,0:T(8,128)(2,1)S(1)} collective-permute-done((bf16[2,128,128]{2,1,0:T(8,128)(2,1)S(1)}, bf16[2,128,128]{2,1,0:T(8,128)(2,1)S(1)}, u32[]{:S(2)}, u32[]{:S(2)}) %collective-permute-start.8) | collective-permute-done | bytes 65568 | tf_op jit(solution)/shard_map/ppermute | solution.py:523
  44.8 0.0 collective-permute-done.7.refs_1_
  44.8 0.0 collective-permute-done.10.refs_5_
  44.8 4.3 %shard_map.95 = bf16[2,27,64,128]{3,2,1,0:T(8,128)(2,1)} custom-call(s32[1]{0:T(128)} %bitcast.place_ref, s32[1]{0:T(128)} %bitcast.1.chip_ref, s32[1]{0:T(128)} %bitcast.2.core_ref, s32[1]{0:T(128)} %bitcast.3.tm_ref, bf16[2,128,128]{2,1,0:T(8,128)(2,1)S(1)} %shard_map.93.refs_0_, bf16[2,128,128]{2,1,0:T(8,128)(2,1)S(1)} %collective-permute-done.7.refs_1_, ...), custom_call_target="tpu_custom_call" | custom-call | tf_op jit(solution)/shard_map/pallas_call | solution.py:672
  (16 shorter events, 0.0 us)
Async XLA Ops:
  0.0 7.4 %collective-permute-start.1 = (f32[2,64,128]{2,1,0:T(8,128)}, f32[2,64,128]{2,1,0:T(8,128)S(1)}, u32[]{:S(2)}, u32[]{:S(2)}) collective-permute-start(f32[2,64,128]{2,1,0:T(8,128)} %bitcast.20), channel_id=1, source_target_pairs={{0,8},{8,0},{16,24},{24,16},{1,9},{9,1},{17,25},{25,17},{2,10},{10... | collective-permute-start | bytes 196616 | tf_op jit(solution)/shard_map/ppermute | solution.py:536
  3.0 4.4 %copy-start.2 = (f32[2,128,64]{1,2,0:T(8,128)S(1)}, f32[2,128,64]{1,2,0:T(8,128)}, u32[]{:S(2)}) copy-start(f32[2,128,64]{1,2,0:T(8,128)} %param.15) | copy-start | bytes 196612
  3.0 12.0 %copy-start = (bf16[1,4,16,16,512]{4,3,2,1,0:T(8,128)(2,1)S(1)}, bf16[1,4,16,16,512]{4,3,2,1,0:T(8,128)(2,1)}, u32[]{:S(2)}) copy-start(bf16[1,4,16,16,512]{4,3,2,1,0:T(8,128)(2,1)} %param.9) | copy-start | bytes 3145732
  3.0 12.0 %copy-start.3 = (bf16[576,16]{1,0:T(8,128)(2,1)S(1)}, bf16[576,16]{1,0:T(8,128)(2,1)}, u32[]{:S(2)}) copy-start(bf16[576,16]{1,0:T(8,128)(2,1)} %constant.19.clone.spread_ref) | copy-start | bytes 55300
  3.0 12.0 %copy-start.4 = (bf16[128,128]{1,0:T(8,128)(2,1)S(1)}, bf16[128,128]{1,0:T(8,128)(2,1)}, u32[]{:S(2)}) copy-start(bf16[128,128]{1,0:T(8,128)(2,1)} %constant.18.clone.pick_any.pick_ref) | copy-start | bytes 98308
  3.0 12.0 %copy-start.5 = (bf16[1,1,4,4,512]{4,3,2,1,0:T(4,128)(2,1)S(1)}, bf16[1,1,4,4,512]{4,3,2,1,0:T(4,128)(2,1)}, u32[]{:S(2)}) copy-start(bf16[1,1,4,4,512]{4,3,2,1,0:T(4,128)(2,1)} %param.12) | copy-start | bytes 49156
  7.4 13.1 %collective-permute-start.2 = (f32[2,2,64,128]{3,2,1,0:T(8,128)S(1)}, f32[2,2,64,128]{3,2,1,0:T(8,128)S(1)}, u32[]{:S(2)}, u32[]{:S(2)}) collective-permute-start(f32[2,2,64,128]{3,2,1,0:T(8,128)S(1)} %pad_maximum_fusion.1), channel_id=1, source_target_pairs={{0,16},{8,24},{16,0},{24,8},{1,17},{9,25},{17,1},{25,9},{2,18},{10... | collective-permute-start | bytes 393224 | tf_op jit(solution)/shard_map/ppermute | solution.py:545
  10.1 5.0 %collective-permute-start = (f32[128,128]{1,0:T(8,128)}, f32[128,128]{1,0:T(8,128)S(1)}, u32[]{:S(2)}, u32[]{:S(2)}) collective-permute-start(f32[128,128]{1,0:T(8,128)} %get-tuple-element.21), channel_id=1, source_target_pairs={{0,1},{1,0},{2,3},{3,2},{4,5},{5,4},{6,7},{7,6},{8,9},{9,8},{10,11... | collective-permute-start | bytes 196616 | tf_op jit(solution)/shard_map/ppermute | solution.py:605
  11.6 13.1 %collective-permute-start.5 = (bf16[1088,128]{1,0:T(8,128)(2,1)}, bf16[1088,128]{1,0:T(8,128)(2,1)S(1)}, u32[]{:S(2)}, u32[]{:S(2)}) collective-permute-start(bf16[1088,128]{1,0:T(8,128)(2,1)} %get-tuple-element.26), channel_id=1, source_target_pairs={{0,5},{1,4},{4,1},{5,0},{2,7},{3,6},{6,3},{7,2},{8,13},{9,12},{12,... | collective-permute-start | bytes 835592 | tf_op jit(solution)/shard_map/ppermute | solution.py:523
  13.0 14.0 %collective-permute-start.4 = (bf16[1088,128]{1,0:T(8,128)(2,1)}, bf16[1088,128]{1,0:T(8,128)(2,1)S(1)}, u32[]{:S(2)}, u32[]{:S(2)}) collective-permute-start(bf16[1088,128]{1,0:T(8,128)(2,1)} %get-tuple-element.26), channel_id=1, source_target_pairs={{0,4},{1,5},{4,0},{5,1},{2,6},{3,7},{6,2},{7,3},{8,12},{9,13},{12,... | collective-permute-start | bytes 835592 | tf_op jit(solution)/shard_map/ppermute | solution.py:523
  13.5 13.8 %collective-permute-start.3 = (bf16[1088,128]{1,0:T(8,128)(2,1)}, bf16[1088,128]{1,0:T(8,128)(2,1)S(1)}, u32[]{:S(2)}, u32[]{:S(2)}) collective-permute-start(bf16[1088,128]{1,0:T(8,128)(2,1)} %get-tuple-element.26), channel_id=1, source_target_pairs={{0,1},{1,0},{4,5},{5,4},{2,3},{3,2},{6,7},{7,6},{8,9},{9,8},{12,13... | collective-permute-start | bytes 835592 | tf_op jit(solution)/shard_map/ppermute | solution.py:523
  15.1 12.3 %copy-start.6 = (bf16[1088,128]{1,0:T(8,128)(2,1)S(1)}, bf16[1088,128]{1,0:T(8,128)(2,1)}, u32[]{:S(2)}) copy-start(bf16[1088,128]{1,0:T(8,128)(2,1)} %get-tuple-element.26) | copy-start | bytes 835588
  20.5 12.9 %all-to-all-start = ((bf16[16,2,32,128]{3,2,1,0:T(8,128)(2,1)}), bf16[16,2,32,128]{3,2,1,0:T(8,128)(2,1)S(1)}, u32[]{:S(2)}, u32[]{:S(2)}) async-start(bf16[16,2,32,128]{3,2,1,0:T(8,128)(2,1)} %bitcast.9), calls=%async_computation | async-start | bytes 524288 | tf_op jit(solution)/shard_map/all_to_all | solution.py:656
  27.3 10.9 %copy-start.7 = (f32[2,27,27]{2,0,1:T(2,128)S(1)}, f32[2,27,27]{2,0,1:T(2,128)}, u32[]{:S(2)}) copy-start(f32[2,27,27]{2,0,1:T(2,128)} %param.13) | copy-start | bytes 17500
  27.5 17.3 %copy-start.1 = (f32[2,128,512]{2,1,0:T(8,128)S(1)}, f32[2,128,512]{2,1,0:T(8,128)}, u32[]{:S(2)}) copy-start(f32[2,128,512]{2,1,0:T(8,128)} %refs_6_.1) | copy-start | bytes 1572868
  33.5 1.5 %collective-permute-start.6 = (bf16[4,4,2,32,128]{4,3,2,1,0:T(8,128)(2,1)S(1)}, bf16[4,4,2,32,128]{4,3,2,1,0:T(8,128)(2,1)S(1)}, u32[]{:S(2)}, u32[]{:S(2)}) collective-permute-start(bf16[4,4,2,32,128]{4,3,2,1,0:T(8,128)(2,1)S(1)} %bitcast.18), channel_id=1, source_target_pairs={{0,2},{2,0},{1,3},{3,1},{4,6},{6,4},{5,7},{7,5},{8,10},{10,8},{9,1... | collective-permute-start | bytes 786440 | tf_op jit(solution)/shard_map/ppermute | solution.py:523
  35.5 9.3 %collective-permute-start.10 = (bf16[4,1088,128]{2,1,0:T(8,128)(2,1)S(1)}, bf16[4,1088,128]{2,1,0:T(8,128)(2,1)S(1)}, u32[]{:S(2)}, u32[]{:S(2)}) collective-permute-start(bf16[4,1088,128]{2,1,0:T(8,128)(2,1)S(1)} %pad_maximum_fusion.refs_4_), channel_id=1, source_target_pairs={{0,2},{2,0},{1,3},{3,1},{4,6},{6,4},{5,7},{7,5},{8,10},{10,8},{9,1... | collective-permute-start | bytes 3342344 | tf_op jit(solution)/shard_map/ppermute | solution.py:523
  35.7 4.4 %collective-permute-start.9 = (bf16[2,128,128]{2,1,0:T(8,128)(2,1)S(1)}, bf16[2,128,128]{2,1,0:T(8,128)(2,1)S(1)}, u32[]{:S(2)}, u32[]{:S(2)}) collective-permute-start(bf16[2,128,128]{2,1,0:T(8,128)(2,1)S(1)} %shard_map.93.refs_0_), channel_id=1, source_target_pairs={{0,24},{8,0},{16,8},{24,16},{1,25},{9,1},{17,9},{25,17},{2,26},{10... | collective-permute-start | bytes 196616 | tf_op jit(solution)/shard_map/ppermute | solution.py:523
  36.0 8.8 %collective-permute-start.8 = (bf16[2,128,128]{2,1,0:T(8,128)(2,1)S(1)}, bf16[2,128,128]{2,1,0:T(8,128)(2,1)S(1)}, u32[]{:S(2)}, u32[]{:S(2)}) collective-permute-start(bf16[2,128,128]{2,1,0:T(8,128)(2,1)S(1)} %shard_map.93.refs_0_), channel_id=1, source_target_pairs={{0,16},{8,24},{16,0},{24,8},{1,17},{9,25},{17,1},{25,9},{2,18},{10... | collective-permute-start | bytes 196616 | tf_op jit(solution)/shard_map/ppermute | solution.py:523
  38.2 6.5 %collective-permute-start.7 = (bf16[2,128,128]{2,1,0:T(8,128)(2,1)S(1)}, bf16[2,128,128]{2,1,0:T(8,128)(2,1)S(1)}, u32[]{:S(2)}, u32[]{:S(2)}) collective-permute-start(bf16[2,128,128]{2,1,0:T(8,128)(2,1)S(1)} %shard_map.93.refs_0_), channel_id=1, source_target_pairs={{0,8},{8,16},{16,24},{24,0},{1,9},{9,17},{17,25},{25,1},{2,10},{10... | collective-permute-start | bytes 196616 | tf_op jit(solution)/shard_map/ppermute | solution.py:523

commit v2 on v1

--- a/solution.py
+++ b/solution.py
@@ -213,6 +213,10 @@
         copy.start()
     own_rows = stacked_rows(grad_ref, rows_ref)
     own = spread_rows(spread_ref, own_rows, cells)
+    for frame in range(frames):
+        for line in range(2):
+            lines = x_ref[frame, :, line].reshape(half * side, channels)
+            classes[frame, line, 0], classes[frame, line, 1] = parity_rows(lines, pick_ref[...])
     copies[0, 1].wait()
     copies[0, 2].wait()
     both = None
@@ -221,10 +225,6 @@
         term = dot_nt(own[tap], pair)
         both = term if both is None else both + term
     early, late = both[:, : second.shape[1]], both[:, second.shape[1] :]
-    for frame in range(frames):
-        for line in range(2):
-            lines = x_ref[frame, :, line].reshape(half * side, channels)
-            classes[frame, line, 0], classes[frame, line, 1] = parity_rows(lines, pick_ref[...])
     count = own_rows.shape[0]
     wide = first.shape[2]
     later_rows = jnp.concatenate(

time: 49.4 us -> 49.5 us (level)
  no operation moved by 1% of the time
where the time goes in v2:
time: 49.5 us; the launch traced here: 49.2 us
  starting transfers between devices  17.5 us (35%)
  waiting for transfers between devices  15.8 us (32%)
  Pallas kernels  15.5 us (31%)
    ppermute x8, waiting for transfers between devices, turned(): return lax.ppermute(block, axes, route)  9.76 us
    ppermute x8, starting transfers between devices, turned(): return lax.ppermute(block, axes, route)  6.27 us
    all_to_all x1, waiting for transfers between devices, shards(): lax.all_to_all(acts.reshape(equals * slices, 2, share, wide), ('chip', 't...  6.05 us
    pallas_call x1, Pallas kernels, shards(): pl.pallas_call(functools.partial(hidden_kernel, clip_parts=clip_parts), o...  5.53 us
    pallas_call x1, Pallas kernels, shards(): pl.pallas_call(functools.partial(update_kernel, slices=slices, cores=core...  4.33 us
    pallas_call x1, Pallas kernels, shards(): pl.pallas_call(project_kernel, out_shape=(jax.ShapeDtypeStruct((8 * cells...  4.31 us
    all_to_all x1, starting transfers between devices, shards(): lax.all_to_all(acts.reshape(equals * slices, 2, share, wide), ('chip', 't...  4.09 us
    ppermute x1, starting transfers between devices, first_round(): lax.ppermute(block, 'fsdp', [(i, i ^ 1) for i in range(size)])  3.02 us
  transfers between devices with their start and end apart: 12, of which 6 were waited for; matrix products, arithmetic and copies ran while one was open for 0% of the time, Pallas kernels for 22%

profile of v2, /device:TPU:0, one launch (start us, length us, event | category | flops | bytes accessed | tf_op | source)
XLA Modules:
  0.0 49.2 jit_solution(17910456625214961829)
XLA Ops:
  0.0 3.0 %collective-permute-start.1 = (f32[2,64,128]{2,1,0:T(8,128)}, f32[2,64,128]{2,1,0:T(8,128)S(1)}, u32[]{:S(2)}, u32[]{:S(2)}) collective-permute-start(f32[2,64,128]{2,1,0:T(8,128)} %bitcast.20), channel_id=1, source_target_pairs={{0,8},{8,0},{16,24},{24,16},{1,9},{9,1},{17,25},{25,17},{2,10},{10... | collective-permute-start | bytes 196616 | tf_op jit(solution)/shard_map/ppermute | solution.py:536
  3.0 0.0 copy-start.5
  3.0 4.3 %shard_map.91 = (bf16[1088,128]{1,0:T(8,128)(2,1)}, f32[128,128]{1,0:T(8,128)}) custom-call(bf16[4,8,2,16,512]{4,3,2,1,0:T(8,128)(2,1)} %bitcast.16, f32[2,128,512]{2,1,0:T(8,128)} %refs_6_.1, bf16[4,4,512]{2,1,0:T(4,128)(2,1)} %bitcast.25, bf16[128,128]{1,0:T(8,128)(2,1)} %constant.18.clone.pick_any.pick_ref, bf16[27,512,128]{2,1,0:T(8,128)(2,1)} %first_any.3), custom_call_target="tpu_custom_call" | custom-call | flops 268435456 | bytes 16777216 | tf_op jit(solution)/shard_map/pallas_call | solution.py:579
  7.4 0.0 collective-permute-done.1
  7.4 2.7 %collective-permute-start.2 = (f32[2,2,64,128]{3,2,1,0:T(8,128)S(1)}, f32[2,2,64,128]{3,2,1,0:T(8,128)S(1)}, u32[]{:S(2)}, u32[]{:S(2)}) collective-permute-start(f32[2,2,64,128]{3,2,1,0:T(8,128)S(1)} %pad_maximum_fusion.1), channel_id=1, source_target_pairs={{0,16},{8,24},{16,0},{24,8},{1,17},{9,25},{17,1},{25,9},{2,18},{10... | collective-permute-start | bytes 393224 | tf_op jit(solution)/shard_map/ppermute | solution.py:545
  10.1 1.5 %collective-permute-start = (f32[128,128]{1,0:T(8,128)}, f32[128,128]{1,0:T(8,128)S(1)}, u32[]{:S(2)}, u32[]{:S(2)}) collective-permute-start(f32[128,128]{1,0:T(8,128)} %get-tuple-element.21), channel_id=1, source_target_pairs={{0,1},{1,0},{2,3},{3,2},{4,5},{5,4},{6,7},{7,6},{8,9},{9,8},{10,11... | collective-permute-start | bytes 196616 | tf_op jit(solution)/shard_map/ppermute | solution.py:605
  11.6 1.5 %collective-permute-start.5 = (bf16[1088,128]{1,0:T(8,128)(2,1)}, bf16[1088,128]{1,0:T(8,128)(2,1)S(1)}, u32[]{:S(2)}, u32[]{:S(2)}) collective-permute-start(bf16[1088,128]{1,0:T(8,128)(2,1)} %get-tuple-element.26), channel_id=1, source_target_pairs={{0,5},{1,4},{4,1},{5,0},{2,7},{3,6},{6,3},{7,2},{8,13},{9,12},{12,... | collective-permute-start | bytes 835592 | tf_op jit(solution)/shard_map/ppermute | solution.py:523
  13.0 0.5 %collective-permute-start.4 = (bf16[1088,128]{1,0:T(8,128)(2,1)}, bf16[1088,128]{1,0:T(8,128)(2,1)S(1)}, u32[]{:S(2)}, u32[]{:S(2)}) collective-permute-start(bf16[1088,128]{1,0:T(8,128)(2,1)} %get-tuple-element.26), channel_id=1, source_target_pairs={{0,4},{1,5},{4,0},{5,1},{2,6},{3,7},{6,2},{7,3},{8,12},{9,13},{12,... | collective-permute-start | bytes 835592 | tf_op jit(solution)/shard_map/ppermute | solution.py:523
  13.5 1.5 %collective-permute-start.3 = (bf16[1088,128]{1,0:T(8,128)(2,1)}, bf16[1088,128]{1,0:T(8,128)(2,1)S(1)}, u32[]{:S(2)}, u32[]{:S(2)}) collective-permute-start(bf16[1088,128]{1,0:T(8,128)(2,1)} %get-tuple-element.26), channel_id=1, source_target_pairs={{0,1},{1,0},{4,5},{5,4},{2,3},{3,2},{6,7},{7,6},{8,9},{9,8},{12,13... | collective-permute-start | bytes 835592 | tf_op jit(solution)/shard_map/ppermute | solution.py:523
  15.0 0.0 collective-permute-done.prior_ref.later_ref
  15.1 5.5 %shard_map.92.after_any = bf16[4,4,2,32,128]{4,3,2,1,0:T(8,128)(2,1)} custom-call(s32[1]{0:T(128)} %bitcast.3.tm_ref, bf16[4,8,2,16,512]{4,3,2,1,0:T(8,128)(2,1)S(1)} %bitcast.17, f32[128,128]{1,0:T(8,128)S(1)} %collective-permute-done.prior_ref.later_ref, bf16[4,4,512]{2,1,0:T(4,128)(2,1)S(1)} %bitcast.26, ...), custom_call_target="tpu_custom_call" | custom-call | flops 679477248 | bytes 209715200 | tf_op jit(solution)/shard_map/pallas_call | solution.py:620
  20.6 0.0 collective-permute-done.2.refs_4_
  20.6 4.1 %all-to-all-start = ((bf16[16,2,32,128]{3,2,1,0:T(8,128)(2,1)}), bf16[16,2,32,128]{3,2,1,0:T(8,128)(2,1)S(1)}, u32[]{:S(2)}, u32[]{:S(2)}) async-start(bf16[16,2,32,128]{3,2,1,0:T(8,128)(2,1)} %bitcast.9), calls=%async_computation | async-start | bytes 524288 | tf_op jit(solution)/shard_map/all_to_all | solution.py:656
  24.7 0.0 collective-permute-done.5
  24.7 2.0 %collective-permute-done.4 = bf16[1088,128]{1,0:T(8,128)(2,1)S(1)} collective-permute-done((bf16[1088,128]{1,0:T(8,128)(2,1)}, bf16[1088,128]{1,0:T(8,128)(2,1)S(1)}, u32[]{:S(2)}, u32[]{:S(2)}) %collective-permute-start.4) | collective-permute-done | bytes 278560 | tf_op jit(solution)/shard_map/ppermute | solution.py:523
  26.7 0.6 %collective-permute-done.3 = bf16[1088,128]{1,0:T(8,128)(2,1)S(1)} collective-permute-done((bf16[1088,128]{1,0:T(8,128)(2,1)}, bf16[1088,128]{1,0:T(8,128)(2,1)S(1)}, u32[]{:S(2)}, u32[]{:S(2)}) %collective-permute-start.3) | collective-permute-done | bytes 278560 | tf_op jit(solution)/shard_map/ppermute | solution.py:523
  27.4 0.1 pad_maximum_fusion.refs_4_
  27.5 0.0 copy-start.1
  27.5 6.1 %all-to-all-done = bf16[16,2,32,128]{3,2,1,0:T(8,128)(2,1)S(1)} async-done(((bf16[16,2,32,128]{3,2,1,0:T(8,128)(2,1)}), bf16[16,2,32,128]{3,2,1,0:T(8,128)(2,1)S(1)}, u32[]{:S(2)}, u32[]{:S(2)}) %all-to-all-start) | async-done | bytes 262176 | tf_op jit(solution)/shard_map/all_to_all | solution.py:656
  33.6 0.0 collective-permute-start.6
  33.6 1.5 %collective-permute-done.6.refs_1_ = bf16[4,4,2,32,128]{4,3,2,1,0:T(8,128)(2,1)S(1)} collective-permute-done((bf16[4,4,2,32,128]{4,3,2,1,0:T(8,128)(2,1)S(1)}, bf16[4,4,2,32,128]{4,3,2,1,0:T(8,128)(2,1)S(1)}, u32[]{:S(2)}, u32[]{:S(2)}) %collective-permute-start.6) | collective-permute-done | bytes 262176 | tf_op jit(solution)/shard_map/ppermute | solution.py:523
  35.1 0.5 shard_map.93.refs_0_
  35.6 0.2 collective-permute-start.10
  35.7 0.3 collective-permute-start.9
  36.1 2.2 %collective-permute-start.8 = (bf16[2,128,128]{2,1,0:T(8,128)(2,1)S(1)}, bf16[2,128,128]{2,1,0:T(8,128)(2,1)S(1)}, u32[]{:S(2)}, u32[]{:S(2)}) collective-permute-start(bf16[2,128,128]{2,1,0:T(8,128)(2,1)S(1)} %shard_map.93.refs_0_), channel_id=1, source_target_pairs={{0,16},{8,24},{16,0},{24,8},{1,17},{9,25},{17,1},{25,9},{2,18},{10... | collective-permute-start | bytes 196616 | tf_op jit(solution)/shard_map/ppermute | solution.py:523
  38.3 0.0 collective-permute-start.7
  38.3 0.9 %shard_map.94 = (bf16[256,2048]{1,0:T(8,128)(2,1)S(1)}, bf16[256,256]{1,0:T(8,128)(2,1)S(1)}, bf16[2,2,216,216]{3,2,1,0:T(8,128)(2,1)S(1)}) custom-call(bf16[4,4,2,32,128]{4,3,2,1,0:T(8,128)(2,1)} %shard_map.92.after_any, f32[2,27,27]{2,1,0:T(8,128)S(1)} %copy.10.mix_ref), custom_call_target="tpu_custom_call" | custom-call | bytes 4194304 | tf_op jit(solution)/shard_map/pallas_call | solution.py:644
  39.3 0.9 %collective-permute-done.9.refs_3_ = bf16[2,128,128]{2,1,0:T(8,128)(2,1)S(1)} collective-permute-done((bf16[2,128,128]{2,1,0:T(8,128)(2,1)S(1)}, bf16[2,128,128]{2,1,0:T(8,128)(2,1)S(1)}, u32[]{:S(2)}, u32[]{:S(2)}) %collective-permute-start.9) | collective-permute-done | bytes 65568 | tf_op jit(solution)/shard_map/ppermute | solution.py:523
  40.1 4.8 %collective-permute-done.8.refs_2_ = bf16[2,128,128]{2,1,0:T(8,128)(2,1)S(1)} collective-permute-done((bf16[2,128,128]{2,1,0:T(8,128)(2,1)S(1)}, bf16[2,128,128]{2,1,0:T(8,128)(2,1)S(1)}, u32[]{:S(2)}, u32[]{:S(2)}) %collective-permute-start.8) | collective-permute-done | bytes 65568 | tf_op jit(solution)/shard_map/ppermute | solution.py:523
  44.9 0.0 collective-permute-done.7.refs_1_
  44.9 0.0 collective-permute-done.10.refs_5_
  44.9 4.3 %shard_map.95 = bf16[2,27,64,128]{3,2,1,0:T(8,128)(2,1)} custom-call(s32[1]{0:T(128)} %bitcast.place_ref, s32[1]{0:T(128)} %bitcast.1.chip_ref, s32[1]{0:T(128)} %bitcast.2.core_ref, s32[1]{0:T(128)} %bitcast.3.tm_ref, bf16[2,128,128]{2,1,0:T(8,128)(2,1)S(1)} %shard_map.93.refs_0_, bf16[2,128,128]{2,1,0:T(8,128)(2,1)S(1)} %collective-permute-done.7.refs_1_, ...), custom_call_target="tpu_custom_call" | custom-call | tf_op jit(solution)/shard_map/pallas_call | solution.py:672
  (16 shorter events, 0.0 us)
Async XLA Ops:
  0.0 7.4 %collective-permute-start.1 = (f32[2,64,128]{2,1,0:T(8,128)}, f32[2,64,128]{2,1,0:T(8,128)S(1)}, u32[]{:S(2)}, u32[]{:S(2)}) collective-permute-start(f32[2,64,128]{2,1,0:T(8,128)} %bitcast.20), channel_id=1, source_target_pairs={{0,8},{8,0},{16,24},{24,16},{1,9},{9,1},{17,25},{25,17},{2,10},{10... | collective-permute-start | bytes 196616 | tf_op jit(solution)/shard_map/ppermute | solution.py:536
  3.0 4.4 %copy-start.2 = (f32[2,128,64]{1,2,0:T(8,128)S(1)}, f32[2,128,64]{1,2,0:T(8,128)}, u32[]{:S(2)}) copy-start(f32[2,128,64]{1,2,0:T(8,128)} %param.15) | copy-start | bytes 196612
  3.0 12.0 %copy-start = (bf16[1,4,16,16,512]{4,3,2,1,0:T(8,128)(2,1)S(1)}, bf16[1,4,16,16,512]{4,3,2,1,0:T(8,128)(2,1)}, u32[]{:S(2)}) copy-start(bf16[1,4,16,16,512]{4,3,2,1,0:T(8,128)(2,1)} %param.9) | copy-start | bytes 3145732
  3.0 12.0 %copy-start.3 = (bf16[576,16]{1,0:T(8,128)(2,1)S(1)}, bf16[576,16]{1,0:T(8,128)(2,1)}, u32[]{:S(2)}) copy-start(bf16[576,16]{1,0:T(8,128)(2,1)} %constant.19.clone.spread_ref) | copy-start | bytes 55300
  3.0 12.0 %copy-start.4 = (bf16[128,128]{1,0:T(8,128)(2,1)S(1)}, bf16[128,128]{1,0:T(8,128)(2,1)}, u32[]{:S(2)}) copy-start(bf16[128,128]{1,0:T(8,128)(2,1)} %constant.18.clone.pick_any.pick_ref) | copy-start | bytes 98308
  3.0 12.0 %copy-start.5 = (bf16[1,1,4,4,512]{4,3,2,1,0:T(4,128)(2,1)S(1)}, bf16[1,1,4,4,512]{4,3,2,1,0:T(4,128)(2,1)}, u32[]{:S(2)}) copy-start(bf16[1,1,4,4,512]{4,3,2,1,0:T(4,128)(2,1)} %param.12) | copy-start | bytes 49156
  7.4 13.2 %collective-permute-start.2 = (f32[2,2,64,128]{3,2,1,0:T(8,128)S(1)}, f32[2,2,64,128]{3,2,1,0:T(8,128)S(1)}, u32[]{:S(2)}, u32[]{:S(2)}) collective-permute-start(f32[2,2,64,128]{3,2,1,0:T(8,128)S(1)} %pad_maximum_fusion.1), channel_id=1, source_target_pairs={{0,16},{8,24},{16,0},{24,8},{1,17},{9,25},{17,1},{25,9},{2,18},{10... | collective-permute-start | bytes 393224 | tf_op jit(solution)/shard_map/ppermute | solution.py:545
  10.1 5.0 %collective-permute-start = (f32[128,128]{1,0:T(8,128)}, f32[128,128]{1,0:T(8,128)S(1)}, u32[]{:S(2)}, u32[]{:S(2)}) collective-permute-start(f32[128,128]{1,0:T(8,128)} %get-tuple-element.21), channel_id=1, source_target_pairs={{0,1},{1,0},{2,3},{3,2},{4,5},{5,4},{6,7},{7,6},{8,9},{9,8},{10,11... | collective-permute-start | bytes 196616 | tf_op jit(solution)/shard_map/ppermute | solution.py:605
  11.6 13.2 %collective-permute-start.5 = (bf16[1088,128]{1,0:T(8,128)(2,1)}, bf16[1088,128]{1,0:T(8,128)(2,1)S(1)}, u32[]{:S(2)}, u32[]{:S(2)}) collective-permute-start(bf16[1088,128]{1,0:T(8,128)(2,1)} %get-tuple-element.26), channel_id=1, source_target_pairs={{0,5},{1,4},{4,1},{5,0},{2,7},{3,6},{6,3},{7,2},{8,13},{9,12},{12,... | collective-permute-start | bytes 835592 | tf_op jit(solution)/shard_map/ppermute | solution.py:523
  13.0 13.7 %collective-permute-start.4 = (bf16[1088,128]{1,0:T(8,128)(2,1)}, bf16[1088,128]{1,0:T(8,128)(2,1)S(1)}, u32[]{:S(2)}, u32[]{:S(2)}) collective-permute-start(bf16[1088,128]{1,0:T(8,128)(2,1)} %get-tuple-element.26), channel_id=1, source_target_pairs={{0,4},{1,5},{4,0},{5,1},{2,6},{3,7},{6,2},{7,3},{8,12},{9,13},{12,... | collective-permute-start | bytes 835592 | tf_op jit(solution)/shard_map/ppermute | solution.py:523
  13.5 13.8 %collective-permute-start.3 = (bf16[1088,128]{1,0:T(8,128)(2,1)}, bf16[1088,128]{1,0:T(8,128)(2,1)S(1)}, u32[]{:S(2)}, u32[]{:S(2)}) collective-permute-start(bf16[1088,128]{1,0:T(8,128)(2,1)} %get-tuple-element.26), channel_id=1, source_target_pairs={{0,1},{1,0},{4,5},{5,4},{2,3},{3,2},{6,7},{7,6},{8,9},{9,8},{12,13... | collective-permute-start | bytes 835592 | tf_op jit(solution)/shard_map/ppermute | solution.py:523
  15.1 12.3 %copy-start.6 = (bf16[1088,128]{1,0:T(8,128)(2,1)S(1)}, bf16[1088,128]{1,0:T(8,128)(2,1)}, u32[]{:S(2)}) copy-start(bf16[1088,128]{1,0:T(8,128)(2,1)} %get-tuple-element.26) | copy-start | bytes 835588
  20.6 12.9 %all-to-all-start = ((bf16[16,2,32,128]{3,2,1,0:T(8,128)(2,1)}), bf16[16,2,32,128]{3,2,1,0:T(8,128)(2,1)S(1)}, u32[]{:S(2)}, u32[]{:S(2)}) async-start(bf16[16,2,32,128]{3,2,1,0:T(8,128)(2,1)} %bitcast.9), calls=%async_computation | async-start | bytes 524288 | tf_op jit(solution)/shard_map/all_to_all | solution.py:656
  27.3 11.0 %copy-start.7 = (f32[2,27,27]{2,0,1:T(2,128)S(1)}, f32[2,27,27]{2,0,1:T(2,128)}, u32[]{:S(2)}) copy-start(f32[2,27,27]{2,0,1:T(2,128)} %param.13) | copy-start | bytes 17500
  27.5 17.4 %copy-start.1 = (f32[2,128,512]{2,1,0:T(8,128)S(1)}, f32[2,128,512]{2,1,0:T(8,128)}, u32[]{:S(2)}) copy-start(f32[2,128,512]{2,1,0:T(8,128)} %refs_6_.1) | copy-start | bytes 1572868
  33.6 1.5 %collective-permute-start.6 = (bf16[4,4,2,32,128]{4,3,2,1,0:T(8,128)(2,1)S(1)}, bf16[4,4,2,32,128]{4,3,2,1,0:T(8,128)(2,1)S(1)}, u32[]{:S(2)}, u32[]{:S(2)}) collective-permute-start(bf16[4,4,2,32,128]{4,3,2,1,0:T(8,128)(2,1)S(1)} %bitcast.18), channel_id=1, source_target_pairs={{0,2},{2,0},{1,3},{3,1},{4,6},{6,4},{5,7},{7,5},{8,10},{10,8},{9,1... | collective-permute-start | bytes 786440 | tf_op jit(solution)/shard_map/ppermute | solution.py:523
  35.6 9.3 %collective-permute-start.10 = (bf16[4,1088,128]{2,1,0:T(8,128)(2,1)S(1)}, bf16[4,1088,128]{2,1,0:T(8,128)(2,1)S(1)}, u32[]{:S(2)}, u32[]{:S(2)}) collective-permute-start(bf16[4,1088,128]{2,1,0:T(8,128)(2,1)S(1)} %pad_maximum_fusion.refs_4_), channel_id=1, source_target_pairs={{0,2},{2,0},{1,3},{3,1},{4,6},{6,4},{5,7},{7,5},{8,10},{10,8},{9,1... | collective-permute-start | bytes 3342344 | tf_op jit(solution)/shard_map/ppermute | solution.py:523
  35.7 4.4 %collective-permute-start.9 = (bf16[2,128,128]{2,1,0:T(8,128)(2,1)S(1)}, bf16[2,128,128]{2,1,0:T(8,128)(2,1)S(1)}, u32[]{:S(2)}, u32[]{:S(2)}) collective-permute-start(bf16[2,128,128]{2,1,0:T(8,128)(2,1)S(1)} %shard_map.93.refs_0_), channel_id=1, source_target_pairs={{0,24},{8,0},{16,8},{24,16},{1,25},{9,1},{17,9},{25,17},{2,26},{10... | collective-permute-start | bytes 196616 | tf_op jit(solution)/shard_map/ppermute | solution.py:523
  36.1 8.8 %collective-permute-start.8 = (bf16[2,128,128]{2,1,0:T(8,128)(2,1)S(1)}, bf16[2,128,128]{2,1,0:T(8,128)(2,1)S(1)}, u32[]{:S(2)}, u32[]{:S(2)}) collective-permute-start(bf16[2,128,128]{2,1,0:T(8,128)(2,1)S(1)} %shard_map.93.refs_0_), channel_id=1, source_target_pairs={{0,16},{8,24},{16,0},{24,8},{1,17},{9,25},{17,1},{25,9},{2,18},{10... | collective-permute-start | bytes 196616 | tf_op jit(solution)/shard_map/ppermute | solution.py:523
  38.3 6.5 %collective-permute-start.7 = (bf16[2,128,128]{2,1,0:T(8,128)(2,1)S(1)}, bf16[2,128,128]{2,1,0:T(8,128)(2,1)S(1)}, u32[]{:S(2)}, u32[]{:S(2)}) collective-permute-start(bf16[2,128,128]{2,1,0:T(8,128)(2,1)S(1)} %shard_map.93.refs_0_), channel_id=1, source_target_pairs={{0,8},{8,16},{16,24},{24,0},{1,9},{9,17},{17,25},{25,1},{2,10},{10... | collective-permute-start | bytes 196616 | tf_op jit(solution)/shard_map/ppermute | solution.py:523

commit v3 on v1

--- a/solution.py
+++ b/solution.py
@@ -608,6 +608,7 @@
     right = right_panels.transpose(0, 2, 1)
     right = first_round(right)
     projected, right = lax.optimization_barrier((projected, right))
+    prior, later, right = lax.optimization_barrier((prior, later, right))
     right = later_rounds(right)
     held = jnp.stack(
         [

time: 49.4 us -> 52.1 us (1.055)
  waiting for transfers between devices: 15.8 us -> 18.8 us
    ppermute x1, waiting for transfers between devices: 0.01 us -> 2.98 us  [shards(): prior = later = lax.ppermute(halo, 'tm', [(0, 1), (1, 0)])]
    all_to_all x1, waiting for transfers between devices: 5.96 us -> 6.91 us  [shards(): lax.all_to_all(acts.reshape(equals * slices, 2, share, wide), ('chip', 't...]
    ppermute x8, waiting for transfers between devices: 9.85 us -> 8.9 us  [turned(): return lax.ppermute(block, axes, route)]
  transfers between devices with their start and end apart: 12 -> 12, of which waited for: 6 -> 7; matrix products, arithmetic and copies ran while one was open for 0% -> 0% of each run, Pallas kernels for 22% -> 21%
where the time goes in v3:
time: 52.1 us; the launch traced here: 51.9 us
  waiting for transfers between devices  18.8 us (36%)
  starting transfers between devices  17.3 us (33%)
  Pallas kernels  15.4 us (30%)
    ppermute x8, waiting for transfers between devices, turned(): return lax.ppermute(block, axes, route)  8.9 us
    all_to_all x1, waiting for transfers between devices, shards(): lax.all_to_all(acts.reshape(equals * slices, 2, share, wide), ('chip', 't...  6.91 us
    ppermute x8, starting transfers between devices, turned(): return lax.ppermute(block, axes, route)  6.27 us
    pallas_call x1, Pallas kernels, shards(): pl.pallas_call(functools.partial(hidden_kernel, clip_parts=clip_parts), o...  5.44 us
    pallas_call x1, Pallas kernels, shards(): pl.pallas_call(functools.partial(update_kernel, slices=slices, cores=core...  4.33 us
    pallas_call x1, Pallas kernels, shards(): pl.pallas_call(project_kernel, out_shape=(jax.ShapeDtypeStruct((8 * cells...  4.31 us
    all_to_all x1, starting transfers between devices, shards(): lax.all_to_all(acts.reshape(equals * slices, 2, share, wide), ('chip', 't...  3.84 us
    ppermute x1, starting transfers between devices, first_round(): lax.ppermute(block, 'fsdp', [(i, i ^ 1) for i in range(size)])  3.02 us
  transfers between devices with their start and end apart: 12, of which 7 were waited for; matrix products, arithmetic and copies ran while one was open for 0% of the time, Pallas kernels for 21%

profile of v3, /device:TPU:0, one launch (start us, length us, event | category | flops | bytes accessed | tf_op | source)
XLA Modules:
  0.0 51.9 jit_solution(4207597971922795426)
XLA Ops:
  0.0 3.0 %collective-permute-start.1 = (f32[2,64,128]{2,1,0:T(8,128)}, f32[2,64,128]{2,1,0:T(8,128)S(1)}, u32[]{:S(2)}, u32[]{:S(2)}) collective-permute-start(f32[2,64,128]{2,1,0:T(8,128)} %bitcast.20), channel_id=1, source_target_pairs={{0,8},{8,0},{16,24},{24,16},{1,9},{9,1},{17,25},{25,17},{2,10},{10... | collective-permute-start | bytes 196616 | tf_op jit(solution)/shard_map/ppermute | solution.py:536
  3.0 0.0 copy-start.5
  3.0 4.3 %shard_map.91 = (bf16[1088,128]{1,0:T(8,128)(2,1)}, f32[128,128]{1,0:T(8,128)}) custom-call(bf16[4,8,2,16,512]{4,3,2,1,0:T(8,128)(2,1)} %bitcast.16, f32[2,128,512]{2,1,0:T(8,128)} %refs_6_.1, bf16[4,4,512]{2,1,0:T(4,128)(2,1)} %bitcast.25, bf16[128,128]{1,0:T(8,128)(2,1)} %constant.18.clone.pick_any.pick_ref, bf16[27,512,128]{2,1,0:T(8,128)(2,1)} %first_any.3), custom_call_target="tpu_custom_call" | custom-call | flops 268435456 | bytes 16777216 | tf_op jit(solution)/shard_map/pallas_call | solution.py:579
  7.4 1.6 %collective-permute-start = (f32[128,128]{1,0:T(8,128)}, f32[128,128]{1,0:T(8,128)S(1)}, u32[]{:S(2)}, u32[]{:S(2)}) collective-permute-start(f32[128,128]{1,0:T(8,128)} %get-tuple-element.25), channel_id=1, source_target_pairs={{0,1},{1,0},{2,3},{3,2},{4,5},{5,4},{6,7},{7,6},{8,9},{9,8},{10,11... | collective-permute-start | bytes 196616 | tf_op jit(solution)/shard_map/ppermute | solution.py:605
  8.9 0.0 collective-permute-done.1
  8.9 3.0 %collective-permute-done.prior_ref.later_ref = f32[128,128]{1,0:T(8,128)S(1)} collective-permute-done((f32[128,128]{1,0:T(8,128)}, f32[128,128]{1,0:T(8,128)S(1)}, u32[]{:S(2)}, u32[]{:S(2)}) %collective-permute-start) | collective-permute-done | bytes 65568 | tf_op jit(solution)/shard_map/ppermute | solution.py:605
  11.9 2.7 %collective-permute-start.2 = (f32[2,2,64,128]{3,2,1,0:T(8,128)S(1)}, f32[2,2,64,128]{3,2,1,0:T(8,128)S(1)}, u32[]{:S(2)}, u32[]{:S(2)}) collective-permute-start(f32[2,2,64,128]{3,2,1,0:T(8,128)S(1)} %pad_maximum_fusion.1), channel_id=1, source_target_pairs={{0,16},{8,24},{16,0},{24,8},{1,17},{9,25},{17,1},{25,9},{2,18},{10... | collective-permute-start | bytes 393224 | tf_op jit(solution)/shard_map/ppermute | solution.py:545
  14.6 2.5 %collective-permute-start.5 = (bf16[1088,128]{1,0:T(8,128)(2,1)}, bf16[1088,128]{1,0:T(8,128)(2,1)S(1)}, u32[]{:S(2)}, u32[]{:S(2)}) collective-permute-start(bf16[1088,128]{1,0:T(8,128)(2,1)} %get-tuple-element.34), channel_id=1, source_target_pairs={{0,5},{1,4},{4,1},{5,0},{2,7},{3,6},{6,3},{7,2},{8,13},{9,12},{12,... | collective-permute-start | bytes 835592 | tf_op jit(solution)/shard_map/ppermute | solution.py:523
  17.0 0.5 collective-permute-start.4
  17.5 0.5 %collective-permute-start.3 = (bf16[1088,128]{1,0:T(8,128)(2,1)}, bf16[1088,128]{1,0:T(8,128)(2,1)S(1)}, u32[]{:S(2)}, u32[]{:S(2)}) collective-permute-start(bf16[1088,128]{1,0:T(8,128)(2,1)} %get-tuple-element.34), channel_id=1, source_target_pairs={{0,1},{1,0},{4,5},{5,4},{2,3},{3,2},{6,7},{7,6},{8,9},{9,8},{12,13... | collective-permute-start | bytes 835592 | tf_op jit(solution)/shard_map/ppermute | solution.py:523
  18.1 5.4 %shard_map.92.after_any = bf16[4,4,2,32,128]{4,3,2,1,0:T(8,128)(2,1)} custom-call(s32[1]{0:T(128)} %bitcast.3.tm_ref, bf16[4,8,2,16,512]{4,3,2,1,0:T(8,128)(2,1)S(1)} %bitcast.17, f32[128,128]{1,0:T(8,128)S(1)} %collective-permute-done.prior_ref.later_ref, bf16[4,4,512]{2,1,0:T(4,128)(2,1)S(1)} %bitcast.26, ...), custom_call_target="tpu_custom_call" | custom-call | flops 679477248 | bytes 209715200 | tf_op jit(solution)/shard_map/pallas_call | solution.py:621
  23.5 0.0 collective-permute-done.2.refs_4_
  23.5 3.8 %all-to-all-start = ((bf16[16,2,32,128]{3,2,1,0:T(8,128)(2,1)}), bf16[16,2,32,128]{3,2,1,0:T(8,128)(2,1)S(1)}, u32[]{:S(2)}, u32[]{:S(2)}) async-start(bf16[16,2,32,128]{3,2,1,0:T(8,128)(2,1)} %bitcast.9), calls=%async_computation | async-start | bytes 524288 | tf_op jit(solution)/shard_map/all_to_all | solution.py:657
  27.4 0.0 collective-permute-done.5
  27.4 1.5 %collective-permute-done.4 = bf16[1088,128]{1,0:T(8,128)(2,1)S(1)} collective-permute-done((bf16[1088,128]{1,0:T(8,128)(2,1)}, bf16[1088,128]{1,0:T(8,128)(2,1)S(1)}, u32[]{:S(2)}, u32[]{:S(2)}) %collective-permute-start.4) | collective-permute-done | bytes 278560 | tf_op jit(solution)/shard_map/ppermute | solution.py:523
  28.9 0.3 collective-permute-done.3
  29.2 0.1 pad_maximum_fusion.refs_4_
  29.3 0.0 copy-start.1
  29.3 6.9 %all-to-all-done = bf16[16,2,32,128]{3,2,1,0:T(8,128)(2,1)S(1)} async-done(((bf16[16,2,32,128]{3,2,1,0:T(8,128)(2,1)}), bf16[16,2,32,128]{3,2,1,0:T(8,128)(2,1)S(1)}, u32[]{:S(2)}, u32[]{:S(2)}) %all-to-all-start) | async-done | bytes 262176 | tf_op jit(solution)/shard_map/all_to_all | solution.py:657
  36.2 0.0 collective-permute-start.6
  36.2 1.5 %collective-permute-done.6.refs_1_ = bf16[4,4,2,32,128]{4,3,2,1,0:T(8,128)(2,1)S(1)} collective-permute-done((bf16[4,4,2,32,128]{4,3,2,1,0:T(8,128)(2,1)S(1)}, bf16[4,4,2,32,128]{4,3,2,1,0:T(8,128)(2,1)S(1)}, u32[]{:S(2)}, u32[]{:S(2)}) %collective-permute-start.6) | collective-permute-done | bytes 262176 | tf_op jit(solution)/shard_map/ppermute | solution.py:523
  37.8 0.5 shard_map.93.refs_0_
  38.2 0.2 collective-permute-start.10
  38.4 0.3 collective-permute-start.9
  38.8 2.2 %collective-permute-start.8 = (bf16[2,128,128]{2,1,0:T(8,128)(2,1)S(1)}, bf16[2,128,128]{2,1,0:T(8,128)(2,1)S(1)}, u32[]{:S(2)}, u32[]{:S(2)}) collective-permute-start(bf16[2,128,128]{2,1,0:T(8,128)(2,1)S(1)} %shard_map.93.refs_0_), channel_id=1, source_target_pairs={{0,16},{8,24},{16,0},{24,8},{1,17},{9,25},{17,1},{25,9},{2,18},{10... | collective-permute-start | bytes 196616 | tf_op jit(solution)/shard_map/ppermute | solution.py:523
  41.0 0.0 collective-permute-start.7
  41.0 0.9 %shard_map.94 = (bf16[256,2048]{1,0:T(8,128)(2,1)S(1)}, bf16[256,256]{1,0:T(8,128)(2,1)S(1)}, bf16[2,2,216,216]{3,2,1,0:T(8,128)(2,1)S(1)}) custom-call(bf16[4,4,2,32,128]{4,3,2,1,0:T(8,128)(2,1)} %shard_map.92.after_any, f32[2,27,27]{2,1,0:T(8,128)S(1)} %copy.10.mix_ref), custom_call_target="tpu_custom_call" | custom-call | bytes 4194304 | tf_op jit(solution)/shard_map/pallas_call | solution.py:645
  41.9 0.9 %collective-permute-done.9.refs_3_ = bf16[2,128,128]{2,1,0:T(8,128)(2,1)S(1)} collective-permute-done((bf16[2,128,128]{2,1,0:T(8,128)(2,1)S(1)}, bf16[2,128,128]{2,1,0:T(8,128)(2,1)S(1)}, u32[]{:S(2)}, u32[]{:S(2)}) %collective-permute-start.9) | collective-permute-done | bytes 65568 | tf_op jit(solution)/shard_map/ppermute | solution.py:523
  42.8 4.8 %collective-permute-done.8.refs_2_ = bf16[2,128,128]{2,1,0:T(8,128)(2,1)S(1)} collective-permute-done((bf16[2,128,128]{2,1,0:T(8,128)(2,1)S(1)}, bf16[2,128,128]{2,1,0:T(8,128)(2,1)S(1)}, u32[]{:S(2)}, u32[]{:S(2)}) %collective-permute-start.8) | collective-permute-done | bytes 65568 | tf_op jit(solution)/shard_map/ppermute | solution.py:523
  47.5 0.0 collective-permute-done.7.refs_1_
  47.6 0.0 collective-permute-done.10.refs_5_
  47.6 4.3 %shard_map.95 = bf16[2,27,64,128]{3,2,1,0:T(8,128)(2,1)} custom-call(s32[1]{0:T(128)} %bitcast.place_ref, s32[1]{0:T(128)} %bitcast.1.chip_ref, s32[1]{0:T(128)} %bitcast.2.core_ref, s32[1]{0:T(128)} %bitcast.3.tm_ref, bf16[2,128,128]{2,1,0:T(8,128)(2,1)S(1)} %shard_map.93.refs_0_, bf16[2,128,128]{2,1,0:T(8,128)(2,1)S(1)} %collective-permute-done.7.refs_1_, ...), custom_call_target="tpu_custom_call" | custom-call | tf_op jit(solution)/shard_map/pallas_call | solution.py:673
  (16 shorter events, 0.0 us)
Async XLA Ops:
  0.0 8.9 %collective-permute-start.1 = (f32[2,64,128]{2,1,0:T(8,128)}, f32[2,64,128]{2,1,0:T(8,128)S(1)}, u32[]{:S(2)}, u32[]{:S(2)}) collective-permute-start(f32[2,64,128]{2,1,0:T(8,128)} %bitcast.20), channel_id=1, source_target_pairs={{0,8},{8,0},{16,24},{24,16},{1,9},{9,1},{17,25},{25,17},{2,10},{10... | collective-permute-start | bytes 196616 | tf_op jit(solution)/shard_map/ppermute | solution.py:536
  3.0 8.9 %copy-start.2 = (f32[2,128,64]{1,2,0:T(8,128)S(1)}, f32[2,128,64]{1,2,0:T(8,128)}, u32[]{:S(2)}) copy-start(f32[2,128,64]{1,2,0:T(8,128)} %param.15) | copy-start | bytes 196612
  3.0 15.0 %copy-start = (bf16[1,4,16,16,512]{4,3,2,1,0:T(8,128)(2,1)S(1)}, bf16[1,4,16,16,512]{4,3,2,1,0:T(8,128)(2,1)}, u32[]{:S(2)}) copy-start(bf16[1,4,16,16,512]{4,3,2,1,0:T(8,128)(2,1)} %param.9) | copy-start | bytes 3145732
  3.0 15.0 %copy-start.3 = (bf16[576,16]{1,0:T(8,128)(2,1)S(1)}, bf16[576,16]{1,0:T(8,128)(2,1)}, u32[]{:S(2)}) copy-start(bf16[576,16]{1,0:T(8,128)(2,1)} %constant.19.clone.spread_ref) | copy-start | bytes 55300
  3.0 15.0 %copy-start.4 = (bf16[128,128]{1,0:T(8,128)(2,1)S(1)}, bf16[128,128]{1,0:T(8,128)(2,1)}, u32[]{:S(2)}) copy-start(bf16[128,128]{1,0:T(8,128)(2,1)} %constant.18.clone.pick_any.pick_ref) | copy-start | bytes 98308
  3.0 15.0 %copy-start.5 = (bf16[1,1,4,4,512]{4,3,2,1,0:T(4,128)(2,1)S(1)}, bf16[1,1,4,4,512]{4,3,2,1,0:T(4,128)(2,1)}, u32[]{:S(2)}) copy-start(bf16[1,1,4,4,512]{4,3,2,1,0:T(4,128)(2,1)} %param.12) | copy-start | bytes 49156
  7.4 4.5 %collective-permute-start = (f32[128,128]{1,0:T(8,128)}, f32[128,128]{1,0:T(8,128)S(1)}, u32[]{:S(2)}, u32[]{:S(2)}) collective-permute-start(f32[128,128]{1,0:T(8,128)} %get-tuple-element.25), channel_id=1, source_target_pairs={{0,1},{1,0},{2,3},{3,2},{4,5},{5,4},{6,7},{7,6},{8,9},{9,8},{10,11... | collective-permute-start | bytes 196616 | tf_op jit(solution)/shard_map/ppermute | solution.py:605
  11.9 11.6 %collective-permute-start.2 = (f32[2,2,64,128]{3,2,1,0:T(8,128)S(1)}, f32[2,2,64,128]{3,2,1,0:T(8,128)S(1)}, u32[]{:S(2)}, u32[]{:S(2)}) collective-permute-start(f32[2,2,64,128]{3,2,1,0:T(8,128)S(1)} %pad_maximum_fusion.1), channel_id=1, source_target_pairs={{0,16},{8,24},{16,0},{24,8},{1,17},{9,25},{17,1},{25,9},{2,18},{10... | collective-permute-start | bytes 393224 | tf_op jit(solution)/shard_map/ppermute | solution.py:545
  14.6 12.8 %collective-permute-start.5 = (bf16[1088,128]{1,0:T(8,128)(2,1)}, bf16[1088,128]{1,0:T(8,128)(2,1)S(1)}, u32[]{:S(2)}, u32[]{:S(2)}) collective-permute-start(bf16[1088,128]{1,0:T(8,128)(2,1)} %get-tuple-element.34), channel_id=1, source_target_pairs={{0,5},{1,4},{4,1},{5,0},{2,7},{3,6},{6,3},{7,2},{8,13},{9,12},{12,... | collective-permute-start | bytes 835592 | tf_op jit(solution)/shard_map/ppermute | solution.py:523
  17.0 11.8 %collective-permute-start.4 = (bf16[1088,128]{1,0:T(8,128)(2,1)}, bf16[1088,128]{1,0:T(8,128)(2,1)S(1)}, u32[]{:S(2)}, u32[]{:S(2)}) collective-permute-start(bf16[1088,128]{1,0:T(8,128)(2,1)} %get-tuple-element.34), channel_id=1, source_target_pairs={{0,4},{1,5},{4,0},{5,1},{2,6},{3,7},{6,2},{7,3},{8,12},{9,13},{12,... | collective-permute-start | bytes 835592 | tf_op jit(solution)/shard_map/ppermute | solution.py:523
  17.5 11.6 %collective-permute-start.3 = (bf16[1088,128]{1,0:T(8,128)(2,1)}, bf16[1088,128]{1,0:T(8,128)(2,1)S(1)}, u32[]{:S(2)}, u32[]{:S(2)}) collective-permute-start(bf16[1088,128]{1,0:T(8,128)(2,1)} %get-tuple-element.34), channel_id=1, source_target_pairs={{0,1},{1,0},{4,5},{5,4},{2,3},{3,2},{6,7},{7,6},{8,9},{9,8},{12,13... | collective-permute-start | bytes 835592 | tf_op jit(solution)/shard_map/ppermute | solution.py:523
  18.1 11.1 %copy-start.6 = (bf16[1088,128]{1,0:T(8,128)(2,1)S(1)}, bf16[1088,128]{1,0:T(8,128)(2,1)}, u32[]{:S(2)}) copy-start(bf16[1088,128]{1,0:T(8,128)(2,1)} %get-tuple-element.34) | copy-start | bytes 835588
  23.5 12.7 %all-to-all-start = ((bf16[16,2,32,128]{3,2,1,0:T(8,128)(2,1)}), bf16[16,2,32,128]{3,2,1,0:T(8,128)(2,1)S(1)}, u32[]{:S(2)}, u32[]{:S(2)}) async-start(bf16[16,2,32,128]{3,2,1,0:T(8,128)(2,1)} %bitcast.9), calls=%async_computation | async-start | bytes 524288 | tf_op jit(solution)/shard_map/all_to_all | solution.py:657
  29.2 11.9 %copy-start.7 = (f32[2,27,27]{2,0,1:T(2,128)S(1)}, f32[2,27,27]{2,0,1:T(2,128)}, u32[]{:S(2)}) copy-start(f32[2,27,27]{2,0,1:T(2,128)} %param.13) | copy-start | bytes 17500
  29.3 18.3 %copy-start.1 = (f32[2,128,512]{2,1,0:T(8,128)S(1)}, f32[2,128,512]{2,1,0:T(8,128)}, u32[]{:S(2)}) copy-start(f32[2,128,512]{2,1,0:T(8,128)} %refs_6_.1) | copy-start | bytes 1572868
  36.2 1.5 %collective-permute-start.6 = (bf16[4,4,2,32,128]{4,3,2,1,0:T(8,128)(2,1)S(1)}, bf16[4,4,2,32,128]{4,3,2,1,0:T(8,128)(2,1)S(1)}, u32[]{:S(2)}, u32[]{:S(2)}) collective-permute-start(bf16[4,4,2,32,128]{4,3,2,1,0:T(8,128)(2,1)S(1)} %bitcast.18), channel_id=1, source_target_pairs={{0,2},{2,0},{1,3},{3,1},{4,6},{6,4},{5,7},{7,5},{8,10},{10,8},{9,1... | collective-permute-start | bytes 786440 | tf_op jit(solution)/shard_map/ppermute | solution.py:523
  38.2 9.3 %collective-permute-start.10 = (bf16[4,1088,128]{2,1,0:T(8,128)(2,1)S(1)}, bf16[4,1088,128]{2,1,0:T(8,128)(2,1)S(1)}, u32[]{:S(2)}, u32[]{:S(2)}) collective-permute-start(bf16[4,1088,128]{2,1,0:T(8,128)(2,1)S(1)} %pad_maximum_fusion.refs_4_), channel_id=1, source_target_pairs={{0,2},{2,0},{1,3},{3,1},{4,6},{6,4},{5,7},{7,5},{8,10},{10,8},{9,1... | collective-permute-start | bytes 3342344 | tf_op jit(solution)/shard_map/ppermute | solution.py:523
  38.4 4.4 %collective-permute-start.9 = (bf16[2,128,128]{2,1,0:T(8,128)(2,1)S(1)}, bf16[2,128,128]{2,1,0:T(8,128)(2,1)S(1)}, u32[]{:S(2)}, u32[]{:S(2)}) collective-permute-start(bf16[2,128,128]{2,1,0:T(8,128)(2,1)S(1)} %shard_map.93.refs_0_), channel_id=1, source_target_pairs={{0,24},{8,0},{16,8},{24,16},{1,25},{9,1},{17,9},{25,17},{2,26},{10... | collective-permute-start | bytes 196616 | tf_op jit(solution)/shard_map/ppermute | solution.py:523
  38.8 8.8 %collective-permute-start.8 = (bf16[2,128,128]{2,1,0:T(8,128)(2,1)S(1)}, bf16[2,128,128]{2,1,0:T(8,128)(2,1)S(1)}, u32[]{:S(2)}, u32[]{:S(2)}) collective-permute-start(bf16[2,128,128]{2,1,0:T(8,128)(2,1)S(1)} %shard_map.93.refs_0_), channel_id=1, source_target_pairs={{0,16},{8,24},{16,0},{24,8},{1,17},{9,25},{17,1},{25,9},{2,18},{10... | collective-permute-start | bytes 196616 | tf_op jit(solution)/shard_map/ppermute | solution.py:523
  41.0 6.5 %collective-permute-start.7 = (bf16[2,128,128]{2,1,0:T(8,128)(2,1)S(1)}, bf16[2,128,128]{2,1,0:T(8,128)(2,1)S(1)}, u32[]{:S(2)}, u32[]{:S(2)}) collective-permute-start(bf16[2,128,128]{2,1,0:T(8,128)(2,1)S(1)} %shard_map.93.refs_0_), channel_id=1, source_target_pairs={{0,8},{8,16},{16,24},{24,0},{1,9},{9,17},{17,25},{25,1},{2,10},{10... | collective-permute-start | bytes 196616 | tf_op jit(solution)/shard_map/ppermute | solution.py:523
